TPU v7x, 32 devices: a whole 2x2x4 slice. The times are simulated.
32 devices in a mesh: dp: 8 (over z, core), expert: 4 (over y, x).
Axes of the slice: x: 2, y: 2, z: 4, core: 2. Of those that a mesh axis runs over, the one named last changes fastest.
Arguments:
- tokens: bfloat16 [32, 36, 36, 384], P(('dp', 'expert')), may hold values from -6 to 6
- shifts: int32 [32, 2], P(('dp', 'expert')), may hold values from 1 to 11
- routes: int32 [32, 1296, 1], P(('dp', 'expert')), may hold values from 0 to 3
- cotangent: bfloat16 [32, 36, 36, 384], P(('dp', 'expert')), may hold values from -6 to 6
- in_weight: bfloat16 [384, 1152], replicated, may hold values from -0.3125 to 0.3125
- in_bias: float32 [2, 384], replicated, may hold values from -3 to 3
- logit_scale: float32 [12], replicated, may hold values from 1.8 to 2.8
- bias_net_first_weight: float32 [2, 512], replicated, may hold values from -6 to 6
- bias_net_first_bias: float32 [512], replicated, may hold values from -3 to 3
- bias_net_second_weight: float32 [512, 12], replicated, may hold values from -0.125 to 0.125
- out_weight: bfloat16 [384, 384], replicated, may hold values from -0.3125 to 0.3125
- out_bias: float32 [384], replicated, may hold values from -3 to 3
- up_weight: bfloat16 [384, 1536], replicated, may hold values from -0.3125 to 0.3125
- up_bias: float32 [1536], replicated, may hold values from -3 to 3
- down_weight: bfloat16 [1536, 384], replicated, may hold values from -0.15625 to 0.15625
- down_bias: float32 [384], replicated, may hold values from -3 to 3
- router_weight: float32 [384, 4], replicated, may hold values from -0.15625 to 0.15625
- expert_up: bfloat16 [4, 384, 1536], P('expert'), may hold values from -0.3125 to 0.3125
- expert_up_bias: float32 [4, 1536], P('expert'), may hold values from -3 to 3
- expert_down: bfloat16 [4, 1536, 384], P('expert'), may hold values from -0.15625 to 0.15625
- expert_down_bias: float32 [4, 384], P('expert'), may hold values from -3 to 3
- norm_gain: float32 [3, 384], replicated, may hold values from 0.5 to 1.5
- norm_bias: float32 [3, 384], replicated, may hold values from -3 to 3
Outputs:
- result: bfloat16 [32, 36, 36, 384], P(('dp', 'expert'))
- tokens_grad: float32 [32, 36, 36, 384], P(('dp', 'expert'))
- in_weight_grad: float32 [384, 1152], replicated
- in_bias_grad: float32 [2, 384], replicated
- logit_scale_grad: float32 [12], replicated
- table_first_grad: float32 [2, 512], replicated
- table_first_bias_grad: float32 [512], replicated
- table_second_grad: float32 [512, 12], replicated
- out_weight_grad: float32 [384, 384], replicated
- out_bias_grad: float32 [384], replicated
- up_weight_grad: float32 [384, 1536], replicated
- up_bias_grad: float32 [1536], replicated
- down_weight_grad: float32 [1536, 384], replicated
- down_bias_grad: float32 [384], replicated
- router_weight_grad: float32 [384, 4], replicated
- expert_up_grad: float32 [4, 384, 1536], P('expert')
- expert_up_bias_grad: float32 [4, 1536], P('expert')
- expert_down_grad: float32 [4, 1536, 384], P('expert')
- expert_down_bias_grad: float32 [4, 384], P('expert')
- norm_gain_grad: float32 [3, 384], replicated
- norm_bias_grad: float32 [3, 384], replicated
All inputs are finite; a program needn't handle non-finite values.
Results may differ from a plain program's by a relative error of at most 0.025.
Values may be sent and summed in bfloat16 or wider, within the bound.
A program may use at most 320 MiB of HBM per device.

v0:
```python
import jax
import jax.numpy as jnp
from jax import lax
from jax.sharding import PartitionSpec as P

D = 384
ATTENTION_HEADS = 12
WS = 12
SIDE = 36


def matmul(operand, matrix):
    return jnp.dot(operand, matrix, precision=lax.Precision.HIGHEST)


def smooth(values):
    return jax.nn.gelu(values, approximate=False)


def layer_norm(values, scales, offset):
    centered = values - jnp.mean(values, axis=-1, keepdims=True)
    spread = jnp.mean(centered * centered, axis=-1, keepdims=True)
    return centered * lax.rsqrt(spread + 1e-05) * scales + offset


def unit_heads(values):
    shaped = values.reshape(values.shape[:-1] + (ATTENTION_HEADS, D // ATTENTION_HEADS))
    shaped = shaped * lax.rsqrt(1.0 + jnp.sum(shaped * shaped, axis=-1, keepdims=True))
    return shaped.reshape(values.shape)


def to_windows(picture):
    across = SIDE // WS
    shaped = picture.reshape(across, WS, across, WS, picture.shape[-1])
    return shaped.transpose(0, 2, 1, 3, 4).reshape(across * across, WS * WS, picture.shape[-1])


def from_windows(windows):
    across = SIDE // WS
    shaped = windows.reshape(across, across, WS, WS, windows.shape[-1])
    return shaped.transpose(0, 2, 1, 3, 4).reshape(SIDE, SIDE, windows.shape[-1])


def window_mask(offsets):
    places = jnp.arange(SIDE, dtype=jnp.int32)

    def region(amount):
        return jnp.where(places < SIDE - WS, 0, jnp.where(places < SIDE - amount, 1, 2)).astype(
            jnp.int32
        )

    labels = region(offsets[0])[:, None] * 3 + region(offsets[1])[None, :]
    window_labels = to_windows(labels[:, :, None])[:, :, 0]
    matching = window_labels[:, :, None] == window_labels[:, None, :]
    return jnp.where(matching, 0.0, -100.0).astype(jnp.float32)


def relative_bias(bias_net_first_weight, bias_net_first_bias, bias_net_second_weight):
    extent = 2 * WS - 1
    steps_along = (jnp.arange(extent, dtype=jnp.int32) - (WS - 1)).astype(jnp.float32) * (
        8.0 / (WS - 1)
    )
    logged = jnp.sign(steps_along) * jnp.log2(jnp.abs(steps_along) + 1.0) / 3.0
    coords_table = jnp.stack([jnp.repeat(logged, extent), jnp.tile(logged, extent)], axis=1)
    layer_out = smooth(matmul(coords_table, bias_net_first_weight) + bias_net_first_bias)
    values = 16.0 * jax.nn.sigmoid(matmul(layer_out, bias_net_second_weight))
    places = jnp.arange(WS * WS, dtype=jnp.int32)
    rows_at = places // WS
    cols_at = places % WS
    lookup = (rows_at[:, None] - rows_at[None, :] + WS - 1) * extent + (
        cols_at[:, None] - cols_at[None, :] + WS - 1
    )
    picked = jnp.take(values, lookup.reshape(-1), axis=0)
    return picked.T.reshape(ATTENTION_HEADS, WS * WS, WS * WS)


def per_device(
    tokens,
    shifts,
    routes,
    cotangent,
    in_weight,
    in_bias,
    logit_scale,
    bias_net_first_weight,
    bias_net_first_bias,
    bias_net_second_weight,
    out_weight,
    out_bias,
    up_weight,
    up_bias,
    down_weight,
    down_bias,
    router_weight,
    expert_up,
    expert_up_bias,
    expert_down,
    expert_down_bias,
    norm_gain,
    norm_bias,
):
    head_dim = D // ATTENTION_HEADS
    window_area = WS * WS
    across = SIDE // WS
    window_count = across * across
    block_shape = (1, window_count, window_area, ATTENTION_HEADS, head_dim)
    experts_all = router_weight.shape[1]
    local_experts = expert_up.shape[0]
    group_size = lax.axis_size("expert")
    token_count = tokens.shape[0] * SIDE * SIDE
    capacity = (5 * token_count + 4 * experts_all - 1) // (4 * experts_all)
    head_scale = jnp.exp(logit_scale)
    bias_table, table_pull = jax.vjp(
        relative_bias, bias_net_first_weight, bias_net_first_bias, bias_net_second_weight
    )
    complete_bias = jnp.concatenate([in_bias[0], jnp.zeros_like(in_bias[0]), in_bias[1]])

    def attend_block(queries, keys_part, values, mask_block):
        raw_scores = jnp.einsum(
            "nqhd,nkhd->nhqk", queries, keys_part, preferred_element_type=jnp.float32
        )
        scores = (
            raw_scores * head_scale[None, :, None, None] + bias_table[None] + mask_block[:, None]
        )
        row_max = jnp.max(scores, axis=-1, keepdims=True)
        exponent = jnp.exp(scores - row_max)
        row_total = jnp.sum(exponent, axis=-1, keepdims=True)
        softmax_low = (exponent / row_total).astype(jnp.bfloat16)
        mixture = jnp.einsum(
            "nhqk,nkhd->nqhd", softmax_low, values, preferred_element_type=jnp.float32
        )
        return (mixture.astype(jnp.bfloat16), (row_max + jnp.log(row_total))[..., 0])

    def attend_back(queries, keys_part, values, mask_block, log_total, grad_mixture):
        raw_scores = jnp.einsum(
            "nqhd,nkhd->nhqk", queries, keys_part, preferred_element_type=jnp.float32
        )
        scores = (
            raw_scores * head_scale[None, :, None, None] + bias_table[None] + mask_block[:, None]
        )
        softmax_result = jnp.exp(scores - log_total[..., None])
        softmax_low = softmax_result.astype(jnp.bfloat16)
        grad_soft = jnp.einsum(
            "nqhd,nkhd->nhqk", grad_mixture, values, preferred_element_type=jnp.float32
        )
        grad_values = jnp.einsum(
            "nhqk,nqhd->nkhd", softmax_low, grad_mixture, preferred_element_type=jnp.float32
        )
        grad_scores = softmax_result * (
            grad_soft - jnp.sum(softmax_result * grad_soft, axis=-1, keepdims=True)
        )
        scale_part = jnp.sum(grad_scores * raw_scores, axis=(0, 2, 3))
        table_part = jnp.sum(grad_scores, axis=0)
        grad_raw = (grad_scores * head_scale[None, :, None, None]).astype(jnp.bfloat16)
        grad_queries = jnp.einsum(
            "nhqk,nkhd->nqhd", grad_raw, keys_part, preferred_element_type=jnp.float32
        )
        grad_keys = jnp.einsum(
            "nhqk,nqhd->nkhd", grad_raw, queries, preferred_element_type=jnp.float32
        )
        return (grad_queries, grad_keys, grad_values, scale_part, table_part)

    def dense_forward(inputs):
        picture, offsets = inputs
        rolled = jnp.roll(picture, (-offsets[0], -offsets[1]), axis=(0, 1))
        windows = to_windows(rolled).reshape(-1, D)
        joint_rows = jnp.dot(windows, in_weight, preferred_element_type=jnp.float32) + complete_bias
        query_key = joint_rows[:, : 2 * D]
        queries = unit_heads(joint_rows[:, :D]).astype(jnp.bfloat16)
        keys_part = unit_heads(joint_rows[:, D : 2 * D]).astype(jnp.bfloat16)
        values = joint_rows[:, 2 * D :].astype(jnp.bfloat16)
        masks = window_mask(offsets).reshape(1, window_count, window_area, window_area)
        mixture, log_total = lax.map(
            lambda pieces: attend_block(*pieces),
            (
                queries.reshape(block_shape),
                keys_part.reshape(block_shape),
                values.reshape(block_shape),
                masks,
            ),
        )
        mixture = mixture.reshape(-1, D)
        branch = jnp.dot(mixture, out_weight, preferred_element_type=jnp.float32) + out_bias
        normed = layer_norm(branch, norm_gain[0], norm_bias[0])
        restored = jnp.roll(
            from_windows(normed.reshape(-1, window_area, D)), (offsets[0], offsets[1]), axis=(0, 1)
        )
        first_out = (picture.astype(jnp.float32) + restored).reshape(-1, D)
        first_low = first_out.astype(jnp.bfloat16)
        hidden = jnp.dot(first_low, up_weight, preferred_element_type=jnp.float32) + up_bias
        activated = smooth(hidden).astype(jnp.bfloat16)
        second_branch = (
            jnp.dot(activated, down_weight, preferred_element_type=jnp.float32) + down_bias
        )
        second_out = first_out + layer_norm(second_branch, norm_gain[1], norm_bias[1])
        kept_state = (
            windows,
            query_key,
            queries,
            keys_part,
            values,
            log_total,
            mixture,
            branch,
            first_low,
            hidden,
            activated,
            second_branch,
        )
        return (second_out, kept_state)

    def dense_backward(inputs):
        offsets, kept_state, grad_second = inputs
        (
            windows,
            query_key,
            queries,
            keys_part,
            values,
            log_total,
            mixture,
            branch,
            first_low,
            hidden,
            activated,
            second_branch,
        ) = kept_state
        unused_two, pull_two = jax.vjp(layer_norm, second_branch, norm_gain[1], norm_bias[1])
        grad_branch_two, gain_two, offset_two = pull_two(grad_second)
        grad_branch_two = grad_branch_two.astype(jnp.bfloat16)
        down_weight_grad = jnp.dot(activated.T, grad_branch_two, preferred_element_type=jnp.float32)
        down_bias_grad = jnp.sum(grad_branch_two.astype(jnp.float32), axis=0)
        grad_activated = jnp.dot(grad_branch_two, down_weight.T, preferred_element_type=jnp.float32)
        unused_act, pull_act = jax.vjp(smooth, hidden)
        grad_hidden = pull_act(grad_activated)[0].astype(jnp.bfloat16)
        up_weight_grad = jnp.dot(first_low.T, grad_hidden, preferred_element_type=jnp.float32)
        up_bias_grad = jnp.sum(grad_hidden.astype(jnp.float32), axis=0)
        grad_first = grad_second + jnp.dot(
            grad_hidden, up_weight.T, preferred_element_type=jnp.float32
        )
        grad_picture = grad_first.reshape(SIDE, SIDE, D)
        grad_rolled = to_windows(
            jnp.roll(grad_picture, (-offsets[0], -offsets[1]), axis=(0, 1))
        ).reshape(-1, D)
        unused_one, pull_one = jax.vjp(layer_norm, branch, norm_gain[0], norm_bias[0])
        grad_branch, gain_one, offset_one = pull_one(grad_rolled)
        grad_branch = grad_branch.astype(jnp.bfloat16)
        out_weight_grad = jnp.dot(mixture.T, grad_branch, preferred_element_type=jnp.float32)
        out_bias_grad = jnp.sum(grad_branch.astype(jnp.float32), axis=0)
        grad_mixture = jnp.dot(
            grad_branch, out_weight.T, preferred_element_type=jnp.float32
        ).astype(jnp.bfloat16)
        masks = window_mask(offsets).reshape(1, window_count, window_area, window_area)
        grad_queries, grad_keys, grad_values, scale_parts, table_parts = lax.map(
            lambda pieces: attend_back(*pieces),
            (
                queries.reshape(block_shape),
                keys_part.reshape(block_shape),
                values.reshape(block_shape),
                masks,
                log_total,
                grad_mixture.reshape(block_shape),
            ),
        )
        unused_query, pull_query = jax.vjp(unit_heads, query_key[:, :D])
        unused_key, pull_key = jax.vjp(unit_heads, query_key[:, D:])
        grad_joint = jnp.concatenate(
            [
                pull_query(grad_queries.reshape(-1, D))[0],
                pull_key(grad_keys.reshape(-1, D))[0],
                grad_values.reshape(-1, D),
            ],
            axis=1,
        ).astype(jnp.bfloat16)
        in_weight_grad = jnp.dot(windows.T, grad_joint, preferred_element_type=jnp.float32)
        bias_sums = jnp.sum(grad_joint.astype(jnp.float32), axis=0)
        in_bias_grad = jnp.stack([bias_sums[:D], bias_sums[2 * D :]])
        grad_windows = jnp.dot(grad_joint, in_weight.T, preferred_element_type=jnp.float32)
        back_rolled = jnp.roll(
            from_windows(grad_windows.reshape(-1, window_area, D)),
            (offsets[0], offsets[1]),
            axis=(0, 1),
        )
        grad_tokens = grad_picture + back_rolled
        scale_grad = jnp.sum(scale_parts, axis=0) * head_scale
        table_grad = jnp.sum(table_parts, axis=0)
        gain_pair = jnp.stack([gain_one, gain_two])
        offset_pair = jnp.stack([offset_one, offset_two])
        return (
            grad_tokens,
            (
                in_weight_grad,
                in_bias_grad,
                scale_grad,
                table_grad,
                out_weight_grad,
                out_bias_grad,
                up_weight_grad,
                up_bias_grad,
                down_weight_grad,
                down_bias_grad,
                gain_pair,
                offset_pair,
            ),
        )

    seconds, kept_states = lax.map(dense_forward, (tokens, shifts))
    flat_second = seconds.reshape(-1, D)
    logits = matmul(flat_second, router_weight)
    router_probs = jax.nn.softmax(logits, axis=-1)
    chosen = routes.reshape(-1)
    onehot = chosen[:, None] == jnp.arange(experts_all, dtype=jnp.int32)[None, :]
    gate_value = jnp.sum(jnp.where(onehot, router_probs, 0.0), axis=-1)
    running = jnp.cumsum(onehot.astype(jnp.int32), axis=0)
    position = jnp.sum(jnp.where(onehot, running, 0), axis=-1) - 1
    kept_mask = position < capacity
    slot_index = jnp.where(kept_mask, chosen * capacity + position, experts_all * capacity)
    slot_rows = jnp.minimum(slot_index, experts_all * capacity - 1)
    sectioned = (
        jnp.zeros((experts_all * capacity + 1, D), jnp.bfloat16)
        .at[slot_index]
        .set(flat_second.astype(jnp.bfloat16))
    )
    sectioned = sectioned[:-1].reshape(experts_all, capacity, D)
    arrived = lax.all_to_all(sectioned, "expert", split_axis=0, concat_axis=0, tiled=True)
    arranged = arrived.reshape(group_size, local_experts, capacity, D)
    expert_hidden = (
        jnp.einsum("secd,edf->secf", arranged, expert_up, preferred_element_type=jnp.float32)
        + expert_up_bias[None, :, None, :]
    )
    expert_active = smooth(expert_hidden).astype(jnp.bfloat16)
    produced = (
        jnp.einsum("secf,efd->secd", expert_active, expert_down, preferred_element_type=jnp.float32)
        + expert_down_bias[None, :, None, :]
    )
    produced = produced.astype(jnp.bfloat16).reshape(experts_all, capacity, D)
    returned = lax.all_to_all(produced, "expert", split_axis=0, concat_axis=0, tiled=True)
    picked = returned.reshape(-1, D)[slot_rows].astype(jnp.float32)
    moe_branch = jnp.where(kept_mask[:, None], gate_value[:, None] * picked, 0.0)
    moe_normed, pull_three = jax.vjp(layer_norm, moe_branch, norm_gain[2], norm_bias[2])
    final = flat_second + moe_normed
    result = final.astype(jnp.bfloat16).reshape(tokens.shape)
    grad_final = cotangent.reshape(-1, D).astype(jnp.float32)
    grad_moe, gain_three, offset_three = pull_three(grad_final)
    grad_gate = jnp.where(kept_mask, jnp.sum(grad_moe * picked, axis=-1), 0.0)
    grad_picked = jnp.where(kept_mask[:, None], gate_value[:, None] * grad_moe, 0.0).astype(
        jnp.bfloat16
    )
    grad_sectioned = (
        jnp.zeros((experts_all * capacity + 1, D), jnp.bfloat16).at[slot_index].set(grad_picked)
    )
    grad_sectioned = grad_sectioned[:-1].reshape(experts_all, capacity, D)
    grad_produced = lax.all_to_all(
        grad_sectioned, "expert", split_axis=0, concat_axis=0, tiled=True
    ).reshape(group_size, local_experts, capacity, D)
    arranged_back = lax.all_to_all(
        sectioned, "expert", split_axis=0, concat_axis=0, tiled=True
    ).reshape(group_size, local_experts, capacity, D)
    hidden_back = (
        jnp.einsum("secd,edf->secf", arranged_back, expert_up, preferred_element_type=jnp.float32)
        + expert_up_bias[None, :, None, :]
    )
    active_back, pull_expert = jax.vjp(smooth, hidden_back)
    active_back = active_back.astype(jnp.bfloat16)
    expert_down_bias_grad = jnp.sum(grad_produced.astype(jnp.float32), axis=(0, 2))
    expert_down_grad = jnp.einsum(
        "secf,secd->efd", active_back, grad_produced, preferred_element_type=jnp.float32
    )
    grad_active = jnp.einsum(
        "secd,efd->secf", grad_produced, expert_down, preferred_element_type=jnp.float32
    )
    grad_expert_hidden = pull_expert(grad_active)[0].astype(jnp.bfloat16)
    expert_up_bias_grad = jnp.sum(grad_expert_hidden.astype(jnp.float32), axis=(0, 2))
    expert_up_grad = jnp.einsum(
        "secd,secf->edf", arranged_back, grad_expert_hidden, preferred_element_type=jnp.float32
    )
    grad_arranged = jnp.einsum(
        "secf,edf->secd", grad_expert_hidden, expert_up, preferred_element_type=jnp.float32
    ).astype(jnp.bfloat16)
    grad_returned = lax.all_to_all(
        grad_arranged.reshape(experts_all, capacity, D),
        "expert",
        split_axis=0,
        concat_axis=0,
        tiled=True,
    )
    grad_dispatch = jnp.where(
        kept_mask[:, None], grad_returned.reshape(-1, D)[slot_rows].astype(jnp.float32), 0.0
    )
    grad_logits = (grad_gate * gate_value)[:, None] * (onehot.astype(jnp.float32) - router_probs)
    router_weight_grad = matmul(flat_second.T, grad_logits)
    grad_second = grad_final + grad_dispatch + matmul(grad_logits, router_weight.T)
    tokens_grad, dense_parts = lax.map(
        dense_backward, (shifts, kept_states, grad_second.reshape(-1, SIDE * SIDE, D))
    )
    dense_parts = jax.tree.map(lambda stacked: jnp.sum(stacked, axis=0), dense_parts)
    (
        in_weight_grad,
        in_bias_grad,
        logit_scale_grad,
        table_grad,
        out_weight_grad,
        out_bias_grad,
        up_weight_grad,
        up_bias_grad,
        down_weight_grad,
        down_bias_grad,
        gain_pair,
        offset_pair,
    ) = dense_parts
    table_first_grad, table_first_bias_grad, table_second_grad = table_pull(table_grad)
    norm_gain_grad = jnp.concatenate([gain_pair, gain_three[None, :]], axis=0)
    norm_bias_grad = jnp.concatenate([offset_pair, offset_three[None, :]], axis=0)
    (
        in_weight_grad,
        in_bias_grad,
        logit_scale_grad,
        table_first_grad,
        table_first_bias_grad,
        table_second_grad,
        out_weight_grad,
        out_bias_grad,
        up_weight_grad,
        up_bias_grad,
        down_weight_grad,
        down_bias_grad,
        router_weight_grad,
        norm_gain_grad,
        norm_bias_grad,
    ) = lax.psum(
        (
            in_weight_grad,
            in_bias_grad,
            logit_scale_grad,
            table_first_grad,
            table_first_bias_grad,
            table_second_grad,
            out_weight_grad,
            out_bias_grad,
            up_weight_grad,
            up_bias_grad,
            down_weight_grad,
            down_bias_grad,
            router_weight_grad,
            norm_gain_grad,
            norm_bias_grad,
        ),
        ("dp", "expert"),
    )
    expert_up_grad, expert_up_bias_grad, expert_down_grad, expert_down_bias_grad = (
        lax.psum(expert_up_grad.astype(jnp.bfloat16), "dp").astype(jnp.float32),
        lax.psum(expert_up_bias_grad.astype(jnp.bfloat16), "dp").astype(jnp.float32),
        lax.psum(expert_down_grad.astype(jnp.bfloat16), "dp").astype(jnp.float32),
        lax.psum(expert_down_bias_grad.astype(jnp.bfloat16), "dp").astype(jnp.float32),
    )
    return (
        result,
        tokens_grad,
        in_weight_grad,
        in_bias_grad,
        logit_scale_grad,
        table_first_grad,
        table_first_bias_grad,
        table_second_grad,
        out_weight_grad,
        out_bias_grad,
        up_weight_grad,
        up_bias_grad,
        down_weight_grad,
        down_bias_grad,
        router_weight_grad,
        expert_up_grad,
        expert_up_bias_grad,
        expert_down_grad,
        expert_down_bias_grad,
        norm_gain_grad,
        norm_bias_grad,
    )


def solution(mesh):
    placed = (
        P(("dp", "expert"), None, None, None),
        P(("dp", "expert"), None),
        P(("dp", "expert"), None, None),
        P(("dp", "expert"), None, None, None),
        P(),
        P(),
        P(),
        P(),
        P(),
        P(),
        P(),
        P(),
        P(),
        P(),
        P(),
        P(),
        P(),
        P("expert", None, None),
        P("expert", None),
        P("expert", None, None),
        P("expert", None),
        P(),
        P(),
    )
    return jax.shard_map(
        per_device,
        mesh=mesh,
        in_specs=placed,
        out_specs=(
            P(("dp", "expert"), None, None, None),
            P(("dp", "expert"), None, None, None),
            P(),
            P(),
            P(),
            P(),
            P(),
            P(),
            P(),
            P(),
            P(),
            P(),
            P(),
            P(),
            P(),
            P("expert", None, None),
            P("expert", None),
            P("expert", None, None),
            P("expert", None),
            P(),
            P(),
        ),
        check_vma=False,
    )
```

profile of v0, /device:TPU:25, one launch (start us, length us, event | category | flops | bytes accessed | tf_op | source)
XLA Modules:
  0.0 886.0 jit_solution(15883671279099801817)
XLA Ops:
  43.2 6.3 squeeze.107
  67.7 4.6 multiply_convert_fusion.3
  76.1 6.4 squeeze.109
  82.5 5.3 squeeze.108
  87.8 38.8 %gather_fusion = f32[20736,12]{1,0:T(8,128)} fusion(f32[529,12]{1,0:T(8,128)S(1)} %copy.193, s32[21504]{0:T(1024)S(1)} %copy-done.64), kind=kCustom, calls=%fused_computation | custom fusion | bytes 2073600 | tf_op jit(solution)/shard_map/jvp(jit(_take))/gather | solution.py:73
  126.6 12.7 %broadcast_select_fusion = f32[20736,12]{1,0:T(8,128)} fusion(f32[20736,12]{1,0:T(8,128)} %gather_fusion, pred[20736]{0:T(1024)(128)(4,1)S(1)} %compare_and_fusion), kind=kLoop, calls=%fused_computation.76 | loop fusion | flops 248832 | bytes 2011392 | tf_op jit(solution)/shard_map/jvp(jit(_take))/select_n | solution.py:73
  139.3 11.6 %copy.194 = f32[12,144,144]{1,2,0:T(8,128)S(1)} copy(f32[12,144,144]{0,2,1:T(8,128)} %bitcast.287) | data formatting | bytes 1990656 | tf_op jit(solution)/shard_map/while/body/eval_jaxpr/while/body/eval_jaxpr/add | solution.py:123
  150.9 14.6 %fusion.153 = (f32[9,12,144]{2,1,0:T(8,128)S(1)}, f32[9,12,144,144]{2,3,1,0:T(8,128)}) fusion(f32[9,144,144]{1,2,0:T(8,128)} %compare_select_fusion, f32[12,144,144]{1,2,0:T(8,128)S(1)} %copy.194, f32[12]{0:T(128)S(1)} %copy-done.117, bf16[9,144,12,32]{1,0,3,2:T(8,128)(2,1)} %squeeze.109, bf16[9,144,12,32]{1,0,3,2:T(8,128)(2,1)} %squeeze.108), kind=kOutput, calls=%fused_computation.317 | convolution fusion | flops 152269632 | bytes 12752688 | tf_op jit(solution)/shard_map/while/body/eval_jaxpr/while/body/eval_jaxpr/nqhd,nkhd->nhqk/dot_general | solution.py:119
  165.5 10.0 %fusion.4 = f32[9,12,144]{2,1,0:T(8,128)S(1)} fusion(f32[9,12,144]{2,1,0:T(8,128)S(1)} %get-tuple-element.376, f32[9,144,144]{1,2,0:T(8,128)} %compare_select_fusion, f32[12,144,144]{1,2,0:T(8,128)S(1)} %copy.194, f32[9,12,144,144]{2,3,1,0:T(8,128)} %get-tuple-element.377, f32[12]{0:T(128)S(1)} %copy-done.117), kind=kLoop, calls=%fused_computation.17 | loop fusion | flops 11181888 | bytes 10824240 | tf_op jit(solution)/shard_map/while/body/eval_jaxpr/while/body/eval_jaxpr/reduce_sum | solution.py:127
  176.6 8.3 convert_bitcast_fusion.1
  184.9 4.5 copy.197
  189.4 4.3 reshape.977
  207.6 21.3 %multiply_convert_fusion.1 = (bf16[1296,1536]{1,0:T(8,128)(2,1)S(1)}, f32[1296,1536]{1,0:T(8,128)}, f32[1296,1536]{1,0:T(8,128)}) fusion(f32[1536]{0:T(1024)S(1)} %copy-done.134, bf16[384,1536]{1,0:T(8,128)(2,1)S(1)} %copy-done, f32[1296,384]{1,0:T(8,128)} %reshape.980), kind=kOutput, calls=%fused_computation.60 | convolution fusion | flops 1660704768 | bytes 23083008 | tf_op jit(solution)/shard_map/while/body/eval_jaxpr/dot_general | solution.py:190
  236.0 9.2 %scatter_custom_fusion = bf16[1621,384]{1,0:T(8,128)(2,1)} fusion(s32[1296]{0:T(1024)} %get-tuple-element.286, f32[1296,384]{1,0:T(8,128)S(1)} %add_add_fusion.7, bf16[]{:T(256)} %constant.552.clone.1), kind=kCustom, calls=%fused_computation.198 | custom fusion | flops 497664 | bytes 3236096 | tf_op jit(solution)/shard_map/scatter | solution.py:322
  248.0 4.3 all-to-all-start
  252.4 15.3 %all-to-all-done = bf16[4,405,384]{2,1,0:T(8,128)(2,1)} async-done(((bf16[4,405,384]{2,1,0:T(8,128)(2,1)}), bf16[4,405,384]{2,1,0:T(8,128)(2,1)}, u32[]{:S(2)}, u32[]{:S(2)}) %all-to-all-start) | async-done | bytes 1244192 | tf_op jit(solution)/shard_map/all_to_all | solution.py:325
  267.7 4.5 fusion.83
  276.0 24.6 %fusion.79 = bf16[4,405,384]{2,1,0:T(8,128)(2,1)} fusion(f32[384]{0:T(512)S(1)} %reduce.24, bf16[1,1536,384]{2,1,0:T(8,128)(2,1)S(1)} %copy-done.130, f32[4,405,1536]{2,1,0:T(8,128)S(1)} %fusion.83, f32[1536]{0:T(1024)S(1)} %reduce.23), kind=kOutput, calls=%fused_computation.168 | convolution fusion | flops 2076503040 | bytes 12384768 | tf_op jit(solution)/shard_map/secf,efd->secd/dot_general | solution.py:333
  300.6 4.6 all-to-all-start.1
  310.5 10.1 %all-to-all-done.1 = bf16[4,405,384]{2,1,0:T(8,128)(2,1)} async-done(((bf16[4,405,384]{2,1,0:T(8,128)(2,1)}), bf16[4,405,384]{2,1,0:T(8,128)(2,1)}, u32[]{:S(2)}, u32[]{:S(2)}) %all-to-all-start.1) | async-done | bytes 1244192 | tf_op jit(solution)/shard_map/all_to_all | solution.py:337
  322.2 4.9 gather_fusion.1
  337.0 11.4 %scatter_custom_fusion.1 = bf16[1621,384]{1,0:T(8,128)(2,1)} fusion(s32[1296]{0:T(1024)} %get-tuple-element.286, f32[1296,384]{1,0:T(8,128)} %reshape.1011, bf16[1296,384]{1,0:T(8,128)(2,1)S(1)} %gather_fusion.1, f32[1296]{0:T(1024)S(1)} %div.164, f32[1296]{0:T(1024)S(1)} %get-tuple-element.367, f32[384]{0:T(512)S(1)} %copy-done.99, ...), kind=kCustom, calls=%fused_computation.200 | custom fusion | flops 6469632 | bytes 4260688 | tf_op jit(solution)/shard_map/scatter | solution.py:350
  351.3 4.7 all-to-all-start.2
  363.1 8.2 all-to-all-done.2
  371.3 28.2 %fusion.169 = (bf16[1536]{0:T(1024)(128)(2,1)}, bf16[4,1,405,1536]{3,2,0,1:T(8,128)(2,1)S(1)}) fusion(bf16[4,405,384]{2,1,0:T(8,128)(2,1)} %all-to-all-done.2, bf16[1,1536,384]{2,1,0:T(8,128)(2,1)} %param.44, f32[1536]{0:T(1024)S(1)} %copy-done.121, f32[4,405,1536]{2,1,0:T(8,128)} %copy-done.23), kind=kOutput, calls=%fused_computation.330 | convolution fusion | flops 2095163904 | bytes 17362944 | tf_op jit(solution)/shard_map/secd,efd->secf/dot_general | solution.py:369
  410.1 26.8 %fusion.55 = bf16[1,1536,384]{2,1,0:T(8,128)(2,1)} fusion(bf16[4,405,384]{2,1,0:T(8,128)(2,1)} %all-to-all-done.2, f32[4,405,1536]{2,1,0:T(8,128)} %copy-done.23, f32[1536]{0:T(1024)S(1)} %copy-done.121), kind=kOutput, calls=%fused_computation.111 | convolution fusion | flops 2075848704 | bytes 12383232 | tf_op jit(solution)/shard_map/secf,secd->efd/dot_general | solution.py:366
  436.9 4.6 fusion.52
  443.3 5.0 gather_fusion.2
  448.5 5.9 multiply_reduce_fusion.9
  456.7 8.0 convert_reduce_fusion
  491.7 5.3 squeeze.110
  497.1 11.2 %fusion.101 = f32[9,12,144,144]{2,3,1,0:T(8,128)} fusion(bf16[9,144,12,32]{1,0,3,2:T(8,128)(2,1)} %squeeze.110, bf16[9,144,12,32]{1,0,3,2:T(8,128)(2,1)} %squeeze.107), kind=kOutput, calls=%fused_computation.202 | convolution fusion | flops 143327232 | bytes 10948608 | tf_op jit(solution)/shard_map/while/body/eval_jaxpr/while/body/eval_jaxpr/nqhd,nkhd->nhqk/dot_general | solution.py:143
  508.3 12.3 %convert_bitcast_fusion = bf16[9,144,12,32]{1,3,2,0:T(8,128)(2,1)} fusion(f32[9,12,144]{2,1,0:T(8,128)S(1)} %copy-done.83, bf16[9,144,12,32]{1,0,3,2:T(8,128)(2,1)} %squeeze.110, f32[9,12,144,144]{2,3,1,0:T(8,128)} %get-tuple-element.377, f32[9,144,144]{1,2,0:T(8,128)} %compare_select_fusion, f32[12,144,144]{1,2,0:T(8,128)S(1)} %copy-done.20, ...), kind=kOutput, calls=%fused_computation.161 | convolution fusion | flops 155022336 | bytes 12752688 | tf_op jit(solution)/shard_map/while/body/eval_jaxpr/while/body/eval_jaxpr/nhqk,nqhd->nkhd/dot_general | solution.py:146
  520.6 31.1 %fusion.154 = (f32[12,144,144]{1,2,0:T(8,128)}, f32[12]{0:T(128)S(1)}, f32[9,12,144,144]{2,3,1,0:T(8,128)}) fusion(f32[9,12,144,144]{2,3,1,0:T(8,128)} %get-tuple-element.377, f32[9,12,144,144]{2,3,1,0:T(8,128)} %fusion.101, f32[9,12,144]{2,1,0:T(8,128)S(1)} %copy-done.83, f32[9,144,144]{1,2,0:T(8,128)} %compare_select_fusion, ...), kind=kOutput, calls=%fused_computation.318 | output fusion | flops 31119684 | bytes 29673312 | tf_op jit(solution)/shard_map/while/body/eval_jaxpr/while/body/eval_jaxpr/sub | solution.py:150
  551.8 10.1 %convolution_bitcast_fusion.1 = f32[9,144,12,32]{1,3,2,0:T(8,128)} fusion(bf16[9,144,12,32]{1,0,3,2:T(8,128)(2,1)S(1)} %copy-done.22, f32[9,12,144,144]{2,3,1,0:T(8,128)} %get-tuple-element.386, f32[12]{0:T(128)S(1)} %copy-done.118), kind=kOutput, calls=%fused_computation.159 | convolution fusion | flops 147806208 | bytes 11943984 | tf_op jit(solution)/shard_map/while/body/eval_jaxpr/while/body/eval_jaxpr/nhqk,nqhd->nkhd/dot_general | solution.py:158
  561.8 7.6 convolution_bitcast_fusion.2
  569.4 5.3 copy.205
  574.7 5.6 reshape.997
  580.3 5.8 reshape.996
  586.1 7.3 copy.212
  593.3 5.6 reshape.999
  598.9 5.7 reshape.998
  607.6 5.2 reshape.1000
  634.6 5.9 fusion.69
  662.8 14.3 %all-reduce.3 = (bf16[1,1536]{1,0:T(2,128)(2,1)S(1)}, bf16[1,384]{1,0:T(2,128)(2,1)S(1)}) all-reduce(bf16[1,1536]{1,0:T(2,128)(2,1)S(1)} %reduce_sum.526, bf16[1,384]{1,0:T(2,128)(2,1)S(1)} %reduce_sum.531), channel_id=1, replica_groups=mesh['dp'=8,'expert'=4] {'dp'}, use_global_device_ids=true, to_apply=%region_51.53 | all-reduce | flops 1920 | bytes 7680 | tf_op jit(solution)/shard_map/psum | solution.py:452
  701.5 5.7 copy.223
  707.2 112.7 %scatter_custom_fusion.2 = f32[529,12]{1,0:T(8,128)S(1)} fusion(s32[20736]{0:T(1024)} %copy-done.65, f32[20736,12]{1,0:T(8,128)} %copy.223, f32[]{:T(128)} %constant.338.clone.1), kind=kCustom, calls=%fused_computation.221 | custom fusion | flops 248832 | bytes 25904 | tf_op jit(solution)/shard_map/transpose(jvp(jit(_take)))/scatter-add | solution.py:73
  825.0 41.5 %all-reduce.1 = (f32[2,384]{1,0:T(2,128)}, f32[12]{0:T(128)}, f32[2,512]{1,0:T(2,128)}, f32[512]{0:T(512)}, f32[512,12]{0,1:T(8,128)}, /*index=5*/f32[384]{0:T(5...) all-reduce(f32[2,384]{1,0:T(2,128)S(1)} %pad_maximum_fusion.5, ...), channel_id=1, replica_groups=mesh['dp'=8,'expert'=4] {'dp','expert'}, use_global_device_ids=true, to_apply=%region_30.32 | all-reduce | flops 14604 | bytes 116832 | tf_op jit(solution)/shard_map/psum | solution.py:430
  (481 shorter events, 238.3 us)
Async XLA Ops:
  7.2 200.4 %copy-start = (bf16[384,1536]{1,0:T(8,128)(2,1)S(1)}, bf16[384,1536]{1,0:T(8,128)(2,1)}, u32[]{:S(2)}) copy-start(bf16[384,1536]{1,0:T(8,128)(2,1)} %param.37) | copy-start | bytes 3538948
  26.9 8.7 copy-start.135
  26.9 8.7 copy-start.136
  29.8 9.1 %copy-start.69 = (s32[1296]{0:T(1024)}, s32[1296]{0:T(1024)S(1)}, u32[]{:S(2)}) copy-start(s32[1296]{0:T(1024)S(1)} %reduce.20) | copy-start | bytes 15556
  29.9 9.0 %copy-start.113 = (f32[529,1]{0,1:T(1,128)}, f32[529,1]{0,1:T(1,128)S(1)}, u32[]{:S(2)}) copy-start(f32[529,1]{0,1:T(1,128)S(1)} %tile.10) | copy-start | bytes 6352
  30.1 8.8 copy-start.115
  57.1 10.7 %copy-start.15 = (f32[1296,384]{1,0:T(8,128)}, f32[1296,384]{1,0:T(8,128)S(1)}, u32[]{:S(2)}) copy-start(f32[1296,384]{1,0:T(8,128)S(1)} %copy.186) | copy-start | bytes 5971972
  139.3 11.6 %copy-start.117 = (f32[12]{0:T(128)S(1)}, f32[12]{0:T(128)}, u32[]{:S(2)}) copy-start(f32[12]{0:T(128)} %exp.23) | copy-start | bytes 148
  150.9 24.6 %copy-start.19 = (f32[12,144,144]{1,2,0:T(8,128)}, f32[12,144,144]{1,2,0:T(8,128)S(1)}, u32[]{:S(2)}) copy-start(f32[12,144,144]{1,2,0:T(8,128)S(1)} %copy.194) | copy-start | bytes 2985988
  165.5 10.0 %copy-start.46 = (f32[9,12,144]{2,1,0:T(8,128)}, f32[9,12,144]{2,1,0:T(8,128)S(1)}, u32[]{:S(2)}) copy-start(f32[9,12,144]{2,1,0:T(8,128)S(1)} %get-tuple-element.376) | copy-start | bytes 186628
  165.5 11.1 %copy-start.1 = (f32[9,12,144,144]{2,3,1,0:T(8,128)S(1)}, f32[9,12,144,144]{2,3,1,0:T(8,128)}, u32[]{:S(2)}) copy-start(f32[9,12,144,144]{2,3,1,0:T(8,128)} %get-tuple-element.377) | copy-start | bytes 26873860
  196.0 38.3 %copy-start.103 = (f32[384]{0:T(512)}, f32[384]{0:T(512)S(1)}, u32[]{:S(2)}) copy-start(f32[384]{0:T(512)S(1)} %get-tuple-element.397) | copy-start | bytes 4612
  207.6 23.2 %copy-start.131 = (bf16[1536,384]{1,0:T(8,128)(2,1)S(1)}, bf16[1536,384]{1,0:T(8,128)(2,1)}, u32[]{:S(2)}) copy-start(bf16[1536,384]{1,0:T(8,128)(2,1)} %param.39) | copy-start | bytes 3538948
  207.6 23.2 %copy-start.137 = (f32[384]{0:T(512)S(1)}, f32[384]{0:T(512)}, u32[]{:S(2)}) copy-start(f32[384]{0:T(512)} %param.40) | copy-start | bytes 4612
  236.0 71.9 %copy-start.2 = (f32[1296,384]{1,0:T(8,128)}, f32[1296,384]{1,0:T(8,128)S(1)}, u32[]{:S(2)}) copy-start(f32[1296,384]{1,0:T(8,128)S(1)} %add_add_fusion.7) | copy-start | bytes 5971972
  248.0 19.7 %all-to-all-start = ((bf16[4,405,384]{2,1,0:T(8,128)(2,1)}), bf16[4,405,384]{2,1,0:T(8,128)(2,1)}, u32[]{:S(2)}, u32[]{:S(2)}) async-start(bf16[4,405,384]{2,1,0:T(8,128)(2,1)} %reshape.983), calls=%async_computation | async-start | bytes 2506752 | tf_op jit(solution)/shard_map/all_to_all | solution.py:325
  252.3 19.8 %copy-start.120 = (f32[1536]{0:T(1024)}, f32[1536]{0:T(1024)S(1)}, u32[]{:S(2)}) copy-start(f32[1536]{0:T(1024)S(1)} %reduce.23) | copy-start | bytes 18436
  300.6 20.0 %all-to-all-start.1 = ((bf16[4,405,384]{2,1,0:T(8,128)(2,1)}), bf16[4,405,384]{2,1,0:T(8,128)(2,1)}, u32[]{:S(2)}, u32[]{:S(2)}) async-start(bf16[4,405,384]{2,1,0:T(8,128)(2,1)} %fusion.79), calls=%async_computation.1 | async-start | bytes 2506752 | tf_op jit(solution)/shard_map/all_to_all | solution.py:337
  305.3 31.7 %copy-start.90 = (pred[1296]{0:T(1024)(128)(4,1)}, pred[1296]{0:T(1024)(128)(4,1)S(1)}, u32[]{:S(2)}) copy-start(pred[1296]{0:T(1024)(128)(4,1)S(1)} %broadcast_compare_fusion) | copy-start | bytes 3892
  305.4 24.8 %copy-start.92 = (pred[36,36]{1,0:T(8,128)(4,1)}, pred[36,36]{1,0:T(8,128)(4,1)S(1)}, u32[]{:S(2)}) copy-start(pred[36,36]{1,0:T(8,128)(4,1)S(1)} %lt.194) | copy-start | bytes 3892
  310.4 52.7 %copy-start.62 = (f32[1296]{0:T(1024)}, f32[1296]{0:T(1024)S(1)}, u32[]{:S(2)}) copy-start(f32[1296]{0:T(1024)S(1)} %get-tuple-element.353) | copy-start | bytes 15556
  310.5 23.1 %copy-start.67 = (f32[36,36]{1,0:T(8,128)}, f32[36,36]{1,0:T(8,128)S(1)}, u32[]{:S(2)}) copy-start(f32[36,36]{1,0:T(8,128)S(1)} %mul.725) | copy-start | bytes 15556
  310.5 16.6 %copy-start.101 = (s32[2048]{0:T(1024)}, s32[2048]{0:T(1024)S(1)}, u32[]{:S(2)}) copy-start(s32[2048]{0:T(1024)S(1)} %pad_clamp_fusion.1) | copy-start | bytes 24580
  327.1 9.9 %copy-start.6 = (bf16[1296,384]{1,0:T(8,128)(2,1)}, bf16[1296,384]{1,0:T(8,128)(2,1)S(1)}, u32[]{:S(2)}) copy-start(bf16[1296,384]{1,0:T(8,128)(2,1)S(1)} %gather_fusion.1) | copy-start | bytes 2985988
  327.8 9.2 %copy-start.76 = (f32[1296]{0:T(1024)}, f32[1296]{0:T(1024)S(1)}, u32[]{:S(2)}) copy-start(f32[1296]{0:T(1024)S(1)} %broadcast_multiply_fusion.1) | copy-start | bytes 15556
  333.4 15.0 %copy-start.93 = (f32[1296]{0:T(1024)}, f32[1296]{0:T(1024)S(1)}, u32[]{:S(2)}) copy-start(f32[1296]{0:T(1024)S(1)} %get-tuple-element.368) | copy-start | bytes 15556
  333.5 14.9 %copy-start.79 = (f32[36,36]{1,0:T(8,128)}, f32[36,36]{1,0:T(8,128)S(1)}, u32[]{:S(2)}) copy-start(f32[36,36]{1,0:T(8,128)S(1)} %get-tuple-element.363) | copy-start | bytes 15556
  333.5 14.9 %copy-start.80 = (f32[36,36]{1,0:T(8,128)}, f32[36,36]{1,0:T(8,128)S(1)}, u32[]{:S(2)}) copy-start(f32[36,36]{1,0:T(8,128)S(1)} %get-tuple-element.364) | copy-start | bytes 15556
  336.9 11.5 %copy-start.81 = (f32[36,36]{1,0:T(8,128)}, f32[36,36]{1,0:T(8,128)S(1)}, u32[]{:S(2)}) copy-start(f32[36,36]{1,0:T(8,128)S(1)} %negate_multiply_fusion.3) | copy-start | bytes 15556
  348.5 10.5 %copy-start.7 = (f32[1,36,36,384]{3,2,1,0:T(8,128)S(1)}, f32[1,36,36,384]{3,2,1,0:T(8,128)}, u32[]{:S(2)}) copy-start(f32[1,36,36,384]{3,2,1,0:T(8,128)} %reshape.1012) | copy-start | bytes 5971972
  351.3 20.1 %all-to-all-start.2 = ((bf16[4,405,384]{2,1,0:T(8,128)(2,1)}), bf16[4,405,384]{2,1,0:T(8,128)(2,1)}, u32[]{:S(2)}, u32[]{:S(2)}) async-start(bf16[4,405,384]{2,1,0:T(8,128)(2,1)} %reshape.990), calls=%async_computation.2 | async-start | bytes 2506752 | tf_op jit(solution)/shard_map/all_to_all | solution.py:353
  357.6 13.7 %copy-start.121 = (f32[1536]{0:T(1024)S(1)}, f32[1536]{0:T(1024)}, u32[]{:S(2)}) copy-start(f32[1536]{0:T(1024)} %copy-done.120) | copy-start | bytes 18436
  363.1 38.7 %copy-start.51 = (bf16[1,384,1536]{2,1,0:T(8,128)(2,1)S(1)}, bf16[1,384,1536]{2,1,0:T(8,128)(2,1)}, u32[]{:S(2)}) copy-start(bf16[1,384,1536]{2,1,0:T(8,128)(2,1)} %param.42) | copy-start | bytes 3538948
  405.8 35.9 %all-to-all-start.3 = ((bf16[4,405,384]{2,1,0:T(8,128)(2,1)}), bf16[4,405,384]{2,1,0:T(8,128)(2,1)}, u32[]{:S(2)}, u32[]{:S(2)}) async-start(bf16[4,405,384]{2,1,0:T(8,128)(2,1)} %fusion.75), calls=%async_computation.3 | async-start | bytes 2506752 | tf_op jit(solution)/shard_map/all_to_all | solution.py:380
  410.0 456.4 %all-reduce.10.cloned.1.call-start = ((), (), s32[]{:S(2)}) async-start(), calls=%async_computation.5 | async-start | bytes 4718592 | tf_op jit(solution)/shard_map/psum | solution.py:451
  410.1 26.8 %copy-start.141 = (bf16[4,1,405,1536]{3,2,0,1:T(8,128)(2,1)S(1)}, bf16[4,1,405,1536]{3,2,0,1:T(8,128)(2,1)}, u32[]{:S(2)}) copy-start(bf16[4,1,405,1536]{3,2,0,1:T(8,128)(2,1)} %copy-done.140) | copy-start | bytes 14929924
  441.6 429.5 %all-reduce.8.cloned.1.call-start = ((), (), s32[]{:S(2)}) async-start(), calls=%async_computation.4 | async-start | bytes 14155776 | tf_op jit(solution)/shard_map/psum | solution.py:430
  455.5 9.1 %copy-start.54 = (bf16[1296,384]{1,0:T(8,128)(2,1)}, bf16[1296,384]{1,0:T(8,128)(2,1)S(1)}, u32[]{:S(2)}) copy-start(bf16[1296,384]{1,0:T(8,128)(2,1)S(1)} %get-tuple-element.346) | copy-start | bytes 2985988
  497.1 11.2 %copy-start.20 = (f32[12,144,144]{1,2,0:T(8,128)S(1)}, f32[12,144,144]{1,2,0:T(8,128)}, u32[]{:S(2)}) copy-start(f32[12,144,144]{1,2,0:T(8,128)} %copy-done.19) | copy-start | bytes 2985988
  497.1 11.2 %copy-start.83 = (f32[9,12,144]{2,1,0:T(8,128)S(1)}, f32[9,12,144]{2,1,0:T(8,128)}, u32[]{:S(2)}) copy-start(f32[9,12,144]{2,1,0:T(8,128)} %log_add_fusion) | copy-start | bytes 186628
  497.1 11.2 %copy-start.118 = (f32[12]{0:T(128)S(1)}, f32[12]{0:T(128)}, u32[]{:S(2)}) copy-start(f32[12]{0:T(128)} %exp.23) | copy-start | bytes 148
  520.6 31.1 %copy-start.22 = (bf16[9,144,12,32]{1,0,3,2:T(8,128)(2,1)S(1)}, bf16[9,144,12,32]{1,0,3,2:T(8,128)(2,1)}, u32[]{:S(2)}) copy-start(bf16[9,144,12,32]{1,0,3,2:T(8,128)(2,1)} %squeeze.108) | copy-start | bytes 2985988
  551.7 10.1 %copy-start.21 = (bf16[9,144,12,32]{1,0,3,2:T(8,128)(2,1)S(1)}, bf16[9,144,12,32]{1,0,3,2:T(8,128)(2,1)}, u32[]{:S(2)}) copy-start(bf16[9,144,12,32]{1,0,3,2:T(8,128)(2,1)} %squeeze.109) | copy-start | bytes 2985988
  701.5 118.7 %copy-start.123 = (f32[1,384]{1,0:T(1,128)S(1)}, f32[1,384]{1,0:T(1,128)}, u32[]{:S(2)}) copy-start(f32[1,384]{1,0:T(1,128)} %reshape.1009) | copy-start | bytes 4612
  701.5 118.7 %copy-start.124 = (f32[1,384]{1,0:T(1,128)S(1)}, f32[1,384]{1,0:T(1,128)}, u32[]{:S(2)}) copy-start(f32[1,384]{1,0:T(1,128)} %reshape.1006) | copy-start | bytes 4612
  701.5 118.7 %copy-start.139 = (f32[12]{0:T(128)S(1)}, f32[12]{0:T(128)}, u32[]{:S(2)}) copy-start(f32[12]{0:T(128)} %param.31) | copy-start | bytes 148
  701.5 118.8 %copy-start.82 = (f32[529,12]{0,1:T(8,128)S(1)}, f32[529,12]{0,1:T(8,128)}, u32[]{:S(2)}) copy-start(f32[529,12]{0,1:T(8,128)} %get-tuple-element.375) | copy-start | bytes 76180
  701.5 118.8 %copy-start.106 = (f32[512,12]{0,1:T(8,128)S(1)}, f32[512,12]{0,1:T(8,128)}, u32[]{:S(2)}) copy-start(f32[512,12]{0,1:T(8,128)} %param.34) | copy-start | bytes 73732
  (104 other events, 343.0 us)
Sparse Core Ops, SparseCore 0:
  441.7 65.6 all-reduce.9
  652.8 166.8 all-reduce.7
where the time goes:
time: 895 us; the launch traced here: 886 us
  local copies, waits for them, and re-layouts  275 us (31%)
  other arithmetic  254 us (28%)
  matrix products  229 us (26%)
  blocking collectives  55.7 us (6%)
  waiting for transfers between devices  33.7 us (4%)
  between operations  20.4 us (2%)
  starting transfers between devices  18 us (2%)
    scatter-add x1, other arithmetic, relative_bias(): picked = jnp.take(values, lookup.reshape(-1), axis=0)  113 us
    psum x1, blocking collectives, per_device(): lax.psum((in_weight_grad, in_bias_grad, logit_scale_grad, table_first_gra...  41.5 us
    gather x1, local copies, waits for them, and re-layouts, relative_bias(): picked = jnp.take(values, lookup.reshape(-1), axis=0)  38.8 us
    sub x1, other arithmetic, attend_back(): grad_soft - jnp.sum(softmax_result * grad_soft, axis=-1, keepdims=True)  31.1 us
    reshape x6, local copies, waits for them, and re-layouts, unit_heads(): return shaped.reshape(values.shape)  28.6 us
    unnamed x297, local copies, waits for them, and re-layouts  28.3 us
    dot_general x1, matrix products, per_device(): jnp.einsum('secd,efd->secf', grad_produced, expert_down, preferred_elemen...  28.2 us
    dot_general x1, matrix products, per_device(): jnp.einsum('secf,secd->efd', active_back, grad_produced, preferred_elemen...  26.8 us
  transfers between devices with their start and end apart: 6, of which 3 were waited for; matrix products, arithmetic and copies ran while one was open for 46% of the time, Pallas kernels for 0%

commit v1 on v0

v1 whole, which is shorter than its diff:
```python
import functools

import jax
import jax.numpy as jnp
from jax import lax
from jax.experimental import pallas as pl
from jax.experimental.pallas import tpu as pltpu
from jax.sharding import PartitionSpec as P

D = 384
HEADS = 12
HEAD = D // HEADS
WS = 12
SIDE = 36
AREA = WS * WS
ACROSS = SIDE // WS
WINDOWS = ACROSS * ACROSS
TOKENS = SIDE * SIDE
FF = 1536
EXTENT = 2 * WS - 1
UNITS = 512
TABLE = 640
ROWS = 432
CHUNK = 256
F32 = jnp.float32
BF16 = jnp.bfloat16
I32 = jnp.int32
VMEM_LIMIT = 60 * 1024 * 1024


def dot(left, right, left_dim, right_dim):
    return lax.dot_general(
        left, right, (((left_dim,), (right_dim,)), ((), ())), preferred_element_type=F32
    )


def exact_dot(left, right, left_dim, right_dim):
    return lax.dot_general(
        left,
        right,
        (((left_dim,), (right_dim,)), ((), ())),
        preferred_element_type=F32,
        precision=lax.Precision.HIGHEST,
    )


def split(values):
    high = values.astype(BF16)
    return high, (values - high.astype(F32)).astype(BF16)


def iota(shape, dim):
    return lax.broadcasted_iota(I32, shape, dim)


def gelu_pair(values):
    size = jnp.abs(values)
    t = 1.0 / (1.0 + 0.2316419 * size)
    bell = jnp.exp(-0.5 * values * values) * 0.3989422804014327
    series = t * (
        0.319381530
        + t * (-0.356563782 + t * (1.781477937 + t * (-1.821255978 + t * 1.330274429)))
    )
    tail = series * bell
    phi = jnp.where(values >= 0.0, 1.0 - tail, tail)
    return values * phi, phi + values * bell


def norm_parts(values):
    centered = values - jnp.mean(values, axis=-1, keepdims=True)
    rstd = lax.rsqrt(jnp.mean(centered * centered, axis=-1, keepdims=True) + 1e-05)
    return centered * rstd, rstd


def norm_back(grad_n, n, rstd):
    return rstd * (
        grad_n
        - jnp.mean(grad_n, axis=-1, keepdims=True)
        - n * jnp.mean(grad_n * n, axis=-1, keepdims=True)
    )


def col_sum(values):
    return jnp.sum(values, axis=0, keepdims=True)


def div_ws(values):
    return (values * 171) >> 11


def full(shape, dtype=F32):
    return jax.ShapeDtypeStruct(shape, dtype)


def whole(shape):
    return pl.BlockSpec(shape, lambda *_: (0,) * len(shape))


def smem():
    return pl.BlockSpec(memory_space=pltpu.SMEM)


def params(**more):
    return pltpu.CompilerParams(vmem_limit_bytes=VMEM_LIMIT, **more)


def offsets_row(shape, dim, sign):
    place = iota(shape, dim)
    row = jnp.floor((place.astype(F32) + 0.5) * (1.0 / EXTENT)).astype(I32)
    col = place - row * EXTENT

    def logged(step):
        e = sign * (step - (WS - 1)).astype(F32) * (8.0 / (WS - 1))
        size = jnp.log2(jnp.abs(e) + 1.0) * (1.0 / 3.0)
        return jnp.where(e < 0.0, -size, size)

    return logged(row), logged(col)


def spread_matrix(mirrored):
    token = iota((384, AREA), 1)
    row = div_ws(token)
    lin = row * EXTENT + (token - row * WS)
    if mirrored:
        lin = (WS - 1) * EXTENT + (WS - 1) - lin
    return (iota((384, AREA), 0) == lin).astype(F32)


def prep_kernel(
    capacity, routes, cot, w1, b1, w2, ls, slot_col, slot_row, zbuf, table, scale, flat, u_ref
):
    slots = zbuf.shape[1]
    experts = zbuf.shape[0]
    before = (iota((AREA, AREA), 1) < iota((AREA, AREA), 0)).astype(BF16)
    carry = jnp.zeros((1, 128), F32)
    for block in range(TOKENS // AREA):
        rows = pl.ds(block * AREA, AREA)
        route = routes[rows, :]
        onehot = (route == iota((AREA, 128), 1)).astype(F32)
        ahead = dot(before, onehot.astype(BF16), 1, 0) + carry
        position = jnp.sum(ahead * onehot, axis=1, keepdims=True)
        carry = carry + col_sum(onehot)
        slot = route.astype(F32) * slots + position
        slot_col[rows, :] = jnp.where(position < capacity, slot, -1.0).astype(I32)
    slot_row[...] = jnp.transpose(
        jnp.broadcast_to(slot_col[...].astype(F32), (TOKENS, 128)), (1, 0)
    )[0:1, :].astype(I32)

    for row in range(SIDE):
        flat[row * SIDE : (row + 1) * SIDE, :] = cot[row].astype(F32)
    low = flat[...].astype(BF16)
    for expert in range(experts):
        pick = (iota((slots, TOKENS), 0) + expert * slots == slot_row[...]).astype(BF16)
        zbuf[expert] = dot(pick, low, 1, 0).astype(BF16)

    scale[...] = jnp.exp(ls[...])
    f_row, f_col = offsets_row((UNITS, TABLE), 1, 1.0)
    w1t = jnp.transpose(w1[...], (1, 0))
    b1t = jnp.transpose(b1[...], (1, 0))
    hidden, _ = gelu_pair(w1t[:, 0:1] * f_row + w1t[:, 1:2] * f_col + b1t[:, 0:1])
    values = 16.0 * jax.nn.sigmoid(exact_dot(w2[...], hidden, 0, 0))
    spread = spread_matrix(False).astype(BF16)
    for head in range(HEADS):
        line = jnp.broadcast_to(values[head : head + 1, :], (16, TABLE))
        line = pltpu.roll(line, 0, 1, stride=1, stride_axis=0)
        for key_row in range(WS):
            shift = (EXTENT * key_row - (WS - 1) * EXTENT - (WS - 1)) % TABLE
            rolled = pltpu.roll(line, shift, 1)
            u_ref[key_row * WS : (key_row + 1) * WS, :] = rolled[:WS, :384]
        high, low_part = split(u_ref[...])
        table[head] = dot(high, spread, 1, 0) + dot(low_part, spread, 1, 0)


def prep(routes, cotangent, w1, b1, w2, ls, experts, capacity, slots):
    return pl.pallas_call(
        functools.partial(prep_kernel, capacity),
        out_shape=(
            full((TOKENS, 1), I32),
            full((1, TOKENS), I32),
            full((experts, slots, D), BF16),
            full((HEADS, AREA, AREA)),
            full((1, HEADS)),
        ),
        scratch_shapes=[pltpu.VMEM((TOKENS, D), F32), pltpu.VMEM((AREA, 384), F32)],
        compiler_params=params(),
        name="prep",
    )(routes, cotangent, w1, b1, w2, ls)


def window_labels(window, shift_row, shift_col):
    def labels(shape, dim):
        token = iota(shape, dim)
        row = div_ws(token)
        col = token - row * WS + lax.rem(window, ACROSS) * WS
        row = row + lax.div(window, ACROSS) * WS

        def region(place, shift):
            last = jnp.where(place < SIDE - shift, 1, 2)
            return jnp.where(place < SIDE - WS, 0, last)

        return region(row, shift_row) * 3 + region(col, shift_col)

    return labels((AREA, 1), 0), labels((1, AREA), 1)


def roll_to_windows(read_row, doubled, windows, shift_row, shift_col):
    for row in range(SIDE):
        line = read_row(row)
        doubled[row, :SIDE, :] = line
        doubled[row, SIDE:, :] = line[:WS, :]
    for row in range(SIDE):
        source = row + shift_row
        source = jnp.where(source >= SIDE, source - SIDE, source)
        line = pltpu.roll(doubled[source], SIDE + WS - shift_col, 0)
        for across in range(ACROSS):
            start = ((row // WS) * ACROSS + across) * AREA + (row % WS) * WS
            windows[start : start + WS, :] = line[across * WS : (across + 1) * WS, :]


def roll_to_image(windows, doubled, write_row, shift_row, shift_col):
    for row in range(SIDE):
        for across in range(ACROSS):
            start = ((row // WS) * ACROSS + across) * AREA + (row % WS) * WS
            line = windows[start : start + WS, :]
            doubled[row, across * WS : (across + 1) * WS, :] = line
            if across == ACROSS - 1:
                doubled[row, SIDE:, :] = line
    for row in range(SIDE):
        source = row - shift_row
        source = jnp.where(source < 0, source + SIDE, source)
        write_row(row, pltpu.roll(doubled[source], shift_col, 0)[:SIDE, :])


def attend_kernel(
    shifts, scale, tokens, in_weight, in_bias, table, out_weight, out_bias, gain, offset,
    normed, n_out, rstd_out, joint, probs, mixture, win_t, inverse,
    doubled, windows, in_weight_t, bias_col,
):
    window = pl.program_id(0)
    shift_row, shift_col = shifts[0, 0], shifts[0, 1]

    @pl.when(window == 0)
    def _():
        roll_to_windows(
            lambda row: tokens[row].astype(F32), doubled, windows, shift_row, shift_col
        )
        in_weight_t[...] = jnp.transpose(in_weight[...], (1, 0))
        bias_col[:, 0:2] = jnp.transpose(in_bias[...], (1, 0))

    mine = windows[pl.ds(pl.multiple_of(window * AREA, 16), AREA), :].astype(BF16)
    win_t[0, :D, :] = jnp.transpose(mine, (1, 0))
    win_t[0, D:, :] = (iota((16, AREA), 0) == 0).astype(BF16)
    label_keys, label_queries = window_labels(window, shift_row, shift_col)
    mask = jnp.where(label_keys == label_queries, 0.0, -100.0)
    for head in range(HEADS):
        at = head * HEAD
        query = dot(in_weight_t[at : at + HEAD, :], mine, 1, 1) + bias_col[at : at + HEAD, 0:1]
        key = dot(in_weight_t[D + at : D + at + HEAD, :], mine, 1, 1)
        value = (
            dot(in_weight_t[2 * D + at : 2 * D + at + HEAD, :], mine, 1, 1)
            + bias_col[at : at + HEAD, 1:2]
        ).astype(BF16)
        query_inverse = lax.rsqrt(1.0 + col_sum(query * query))
        key_inverse = lax.rsqrt(1.0 + col_sum(key * key))
        query = (query * query_inverse).astype(BF16)
        key = (key * key_inverse).astype(BF16)
        scores = dot(key, query, 0, 0) * scale[0, head] + (table[head] + mask)
        exponent = jnp.exp(scores - jnp.max(scores, axis=0, keepdims=True))
        low = (exponent * (1.0 / col_sum(exponent))).astype(BF16)
        mixture[0, at : at + HEAD, :] = dot(value, low, 1, 0).astype(BF16)
        probs[0, head] = low
        joint[0, at : at + HEAD, :] = query
        joint[0, D + at : D + at + HEAD, :] = key
        joint[0, 2 * D + at : 2 * D + at + HEAD, :] = value
        inverse[0, head : head + 1, :] = query_inverse
        inverse[0, HEADS + head : HEADS + head + 1, :] = key_inverse
    branch = dot(mixture[0], out_weight[...], 0, 0) + out_bias[...]
    n, rstd = norm_parts(branch)
    normed[...] = n * gain[0:1, :] + offset[0:1, :]
    n_out[...] = n.astype(BF16)
    rstd_out[...] = rstd


def attend(shifts, scale, tokens, in_weight, in_bias, table, out_weight, out_bias, gain, offset):
    per_window = lambda *dims: pl.BlockSpec((1,) + dims, lambda w: (w,) + (0,) * len(dims))
    rows = lambda width: pl.BlockSpec((AREA, width), lambda w: (w, 0))
    return pl.pallas_call(
        attend_kernel,
        grid=(WINDOWS,),
        in_specs=[
            smem(),
            smem(),
            whole((SIDE, SIDE, D)),
            whole((D, 3 * D)),
            whole((2, D)),
            whole((HEADS, AREA, AREA)),
            whole((D, D)),
            whole((1, D)),
            whole((3, D)),
            whole((3, D)),
        ],
        out_specs=(
            rows(D),
            rows(D),
            rows(1),
            per_window(3 * D, AREA),
            per_window(HEADS, AREA, AREA),
            per_window(D, AREA),
            per_window(D + 16, AREA),
            per_window(2 * HEADS, AREA),
        ),
        out_shape=(
            full((TOKENS, D)),
            full((TOKENS, D), BF16),
            full((TOKENS, 1)),
            full((WINDOWS, 3 * D, AREA), BF16),
            full((WINDOWS, HEADS, AREA, AREA), BF16),
            full((WINDOWS, D, AREA), BF16),
            full((WINDOWS, D + 16, AREA), BF16),
            full((WINDOWS, 2 * HEADS, AREA)),
        ),
        scratch_shapes=[
            pltpu.VMEM((SIDE, SIDE + WS, D), F32),
            pltpu.VMEM((TOKENS, D), F32),
            pltpu.VMEM((3 * D, D), BF16),
            pltpu.VMEM((D, 128), F32),
        ],
        compiler_params=params(),
        name="attend",
    )(shifts, scale, tokens, in_weight, in_bias, table, out_weight, out_bias, gain, offset)


def forward_kernel(
    shifts, tokens, normed, up, up_bias, down, down_bias, gain, offset, slot_row,
    first_low, active, slope, n_out, rstd_out, second, buffer,
    doubled, image, second_low,
):
    step = pl.program_id(0)

    @pl.when(step == 0)
    def _():
        def write_row(row, line):
            image[row * SIDE : (row + 1) * SIDE, :] = line + tokens[row].astype(F32)

        roll_to_image(normed, doubled, write_row, shifts[0, 0], shifts[0, 1])

    rows = pl.ds(pl.multiple_of(step * ROWS, 16), ROWS)
    first = image[rows, :]
    low = first.astype(BF16)
    first_low[...] = low
    branch = jnp.broadcast_to(down_bias[...], (ROWS, D))
    for at in range(0, FF, CHUNK):
        hidden = dot(low, up[:, at : at + CHUNK], 1, 0) + up_bias[:, at : at + CHUNK]
        activated, derivative = gelu_pair(hidden)
        activated = activated.astype(BF16)
        active[:, at : at + CHUNK] = activated
        slope[:, at : at + CHUNK] = derivative.astype(BF16)
        branch += dot(activated, down[at : at + CHUNK, :], 1, 0)
    n, rstd = norm_parts(branch)
    n_out[...] = n.astype(BF16)
    rstd_out[...] = rstd
    result = first + n * gain[1:2, :] + offset[1:2, :]
    second[...] = result
    second_low[rows, :] = result.astype(BF16)

    @pl.when(step == TOKENS // ROWS - 1)
    def _():
        slots = buffer.shape[1]
        for expert in range(buffer.shape[0]):
            pick = (iota((slots, TOKENS), 0) + expert * slots == slot_row[...]).astype(BF16)
            buffer[expert] = dot(pick, second_low[...], 1, 0).astype(BF16)


def forward(
    shifts, tokens, normed, up, up_bias, down, down_bias, gain, offset, slot_row, experts, slots
):
    rows = lambda width: pl.BlockSpec((ROWS, width), lambda i: (i, 0))
    return pl.pallas_call(
        forward_kernel,
        grid=(TOKENS // ROWS,),
        in_specs=[
            smem(),
            whole((SIDE, SIDE, D)),
            whole((TOKENS, D)),
            whole((D, FF)),
            whole((1, FF)),
            whole((FF, D)),
            whole((1, D)),
            whole((3, D)),
            whole((3, D)),
            whole((1, TOKENS)),
        ],
        out_specs=(
            rows(D),
            rows(FF),
            rows(FF),
            rows(D),
            rows(1),
            rows(D),
            whole((experts, slots, D)),
        ),
        out_shape=(
            full((TOKENS, D), BF16),
            full((TOKENS, FF), BF16),
            full((TOKENS, FF), BF16),
            full((TOKENS, D), BF16),
            full((TOKENS, 1)),
            full((TOKENS, D)),
            full((experts, slots, D), BF16),
        ),
        scratch_shapes=[
            pltpu.VMEM((SIDE, SIDE + WS, D), F32),
            pltpu.VMEM((TOKENS, D), F32),
            pltpu.VMEM((TOKENS, D), BF16),
        ],
        compiler_params=params(),
        name="forward",
    )(shifts, tokens, normed, up, up_bias, down, down_bias, gain, offset, slot_row)


def expert_kernel(
    arrived, cot, router, up, up_bias, down, down_bias, gain,
    out, grad_in, up_grad, up_bias_grad, down_grad_t, down_bias_grad,
    active, slope, grad_hidden_sum,
):
    source = pl.program_id(0)
    me = lax.axis_index("expert")

    @pl.when(source == 0)
    def _():
        for ref in (up_grad, up_bias_grad, down_grad_t, down_bias_grad):
            ref[...] = jnp.zeros_like(ref)

    features = arrived[0]
    slots = features.shape[0]
    router_high, router_low = split(router[...])
    logits = dot(features, router_high, 1, 0) + dot(features, router_low, 1, 0)
    chances = jnp.exp(logits - jnp.max(logits, axis=1, keepdims=True))
    own = jnp.where(iota(chances.shape, 1) == me, chances, 0.0)
    gate = jnp.sum(own, axis=1, keepdims=True) / jnp.sum(chances, axis=1, keepdims=True)

    output = jnp.broadcast_to(down_bias[...], (slots, D))
    for at in range(0, FF, CHUNK):
        hidden = dot(features, up[:, at : at + CHUNK], 1, 0) + up_bias[:, at : at + CHUNK]
        activated, derivative = gelu_pair(hidden)
        activated = activated.astype(BF16)
        active[:, at : at + CHUNK] = activated
        slope[:, at : at + CHUNK] = derivative
        output += dot(activated, down[at : at + CHUNK, :], 1, 0)
    output = output.astype(BF16)
    out[0] = output
    n, rstd = norm_parts(gate * output.astype(F32))
    grad_output = gate * norm_back(gain[2:3, :] * cot[0].astype(F32), n, rstd)
    grad_low = grad_output.astype(BF16)
    down_bias_grad[...] += col_sum(grad_low.astype(F32))
    grad_low_t = jnp.transpose(grad_low, (1, 0))
    features_t = jnp.transpose(features, (1, 0))
    grad_features = jnp.zeros((slots, D), F32)
    for at in range(0, FF, CHUNK):
        part = slice(at, at + CHUNK)
        grad_hidden = dot(grad_low, down[part, :], 1, 1) * slope[:, part]
        grad_hidden_low = grad_hidden.astype(BF16)
        up_bias_grad[:, part] += col_sum(grad_hidden)
        down_grad_t[:, part] += dot(grad_low_t, active[:, part], 1, 0)
        up_grad[:, part] += dot(features_t, grad_hidden_low, 1, 0)
        grad_features += dot(grad_hidden_low, up[:, part], 1, 1)
    grad_in[0] = grad_features.astype(BF16)


def run_experts(arrived, cot, router, up, up_bias, down, down_bias, gain):
    sources, slots, _ = arrived.shape
    block = pl.BlockSpec((1, slots, D), lambda i: (i, 0, 0))
    return pl.pallas_call(
        expert_kernel,
        grid=(sources,),
        in_specs=[
            block,
            block,
            whole(router.shape),
            whole((D, FF)),
            whole((1, FF)),
            whole((FF, D)),
            whole((1, D)),
            whole((3, D)),
        ],
        out_specs=(
            block,
            block,
            whole((D, FF)),
            whole((1, FF)),
            whole((D, FF)),
            whole((1, D)),
        ),
        out_shape=(
            full((sources, slots, D), BF16),
            full((sources, slots, D), BF16),
            full((D, FF)),
            full((1, FF)),
            full((D, FF)),
            full((1, D)),
        ),
        scratch_shapes=[
            pltpu.VMEM((slots, FF), BF16),
            pltpu.VMEM((slots, FF), F32),
            pltpu.VMEM((8, 128), F32),
        ],
        compiler_params=params(),
        name="experts",
    )(arrived, cot, router, up, up_bias, down, down_bias, gain)


def backward_kernel(
    second, cot, slot_col, routes, outputs, grads, router, first_low, active, slope, n_in, rstd_in,
    up, down, gain, offset,
    result, grad_first, up_grad, up_bias_grad, down_grad_t, down_bias_grad, router_grad,
    gain_grad, offset_grad,
    flat,
):
    step = pl.program_id(0)

    @pl.when(step == 0)
    def _():
        for ref in (
            up_grad, up_bias_grad, down_grad_t, down_bias_grad, router_grad, gain_grad, offset_grad
        ):
            ref[...] = jnp.zeros_like(ref)

    lines = ROWS // SIDE
    for line in range(lines):
        flat[line * SIDE : (line + 1) * SIDE, :] = cot[line].astype(F32)
    z = flat[...]
    x = second[...]
    slots_all = outputs.shape[0]
    pick = (slot_col[...] == iota((ROWS, slots_all), 1)).astype(BF16)
    picked = dot(pick, outputs[...], 1, 0)
    dispatched = dot(pick, grads[...], 1, 0)

    logits = exact_dot(x, router[...], 1, 0)
    chances = jnp.exp(logits - jnp.max(logits, axis=1, keepdims=True))
    chances = chances / jnp.sum(chances, axis=1, keepdims=True)
    onehot = (routes[...] == iota(chances.shape, 1)).astype(F32)
    gate = jnp.sum(chances * onehot, axis=1, keepdims=True)
    n, rstd = norm_parts(gate * picked)
    final = x + n * gain[2:3, :] + offset[2:3, :]
    gain_grad[2:3, :] += col_sum(z * n)
    offset_grad[2:3, :] += col_sum(z)
    grad_moe = norm_back(gain[2:3, :] * z, n, rstd)
    grad_gate = jnp.sum(grad_moe * picked, axis=1, keepdims=True)
    grad_logits = grad_gate * gate * (onehot - chances)
    grad_logits_low = grad_logits.astype(BF16)
    router_grad[...] += dot(x.astype(BF16), grad_logits_low, 0, 0)
    grad_second = z + dispatched + dot(grad_logits_low, router[...].astype(BF16), 1, 1)

    n = n_in[...].astype(F32)
    gain_grad[1:2, :] += col_sum(grad_second * n)
    offset_grad[1:2, :] += col_sum(grad_second)
    grad_branch = norm_back(gain[1:2, :] * grad_second, n, rstd_in[...])
    grad_low = grad_branch.astype(BF16)
    down_bias_grad[...] += col_sum(grad_branch)
    grad_low_t = jnp.transpose(grad_low, (1, 0))
    first_t = jnp.transpose(first_low[...], (1, 0))
    total = jnp.zeros((ROWS, D), F32)
    for at in range(0, FF, CHUNK):
        part = slice(at, at + CHUNK)
        grad_hidden = dot(grad_low, down[part, :], 1, 1) * slope[:, part].astype(F32)
        grad_hidden_low = grad_hidden.astype(BF16)
        up_bias_grad[:, part] += col_sum(grad_hidden)
        down_grad_t[:, part] += dot(grad_low_t, active[:, part], 1, 0)
        up_grad[:, part] += dot(first_t, grad_hidden_low, 1, 0)
        total += dot(grad_hidden_low, up[:, part], 1, 1)
    grad_first[...] = total + grad_second
    flat[...] = final
    for line in range(lines):
        result[line] = flat[line * SIDE : (line + 1) * SIDE, :].astype(BF16)


def backward(
    second, cot, slot_col, routes, outputs, grads, router, first_low, active, slope, n, rstd,
    up, down, gain, offset,
):
    rows = lambda width: pl.BlockSpec((ROWS, width), lambda i: (i, 0))
    lines = pl.BlockSpec((ROWS // SIDE, SIDE, D), lambda i: (i, 0, 0))
    slots_all = outputs.shape[0]
    return pl.pallas_call(
        backward_kernel,
        grid=(TOKENS // ROWS,),
        in_specs=[
            rows(D),
            lines,
            rows(1),
            rows(1),
            whole((slots_all, D)),
            whole((slots_all, D)),
            whole(router.shape),
            rows(D),
            rows(FF),
            rows(FF),
            rows(D),
            rows(1),
            whole((D, FF)),
            whole((FF, D)),
            whole((3, D)),
            whole((3, D)),
        ],
        out_specs=(
            lines,
            rows(D),
            whole((D, FF)),
            whole((1, FF)),
            whole((D, FF)),
            whole((1, D)),
            whole(router.shape),
            whole((3, D)),
            whole((3, D)),
        ),
        out_shape=(
            full((SIDE, SIDE, D), BF16),
            full((TOKENS, D)),
            full((D, FF)),
            full((1, FF)),
            full((D, FF)),
            full((1, D)),
            full(router.shape),
            full((3, D)),
            full((3, D)),
        ),
        scratch_shapes=[pltpu.VMEM((ROWS, D), F32)],
        compiler_params=params(),
        name="backward",
    )(
        second, cot, slot_col, routes, outputs, grads, router, first_low, active, slope, n, rstd,
        up, down, gain, offset,
    )


def attend_back_kernel(
    shifts, scale, grad_first, n_in, rstd_in, joint, probs, mixture, win_t, inverse,
    in_weight, out_weight, gain,
    tokens_grad, in_grad, out_grad, out_bias_grad, gain_grad, offset_grad, scale_grad, table_grad,
    doubled, windows, joint_grad,
):
    window = pl.program_id(0)
    shift_row, shift_col = shifts[0, 0], shifts[0, 1]

    @pl.when(window == 0)
    def _():
        for ref in (
            in_grad, out_grad, out_bias_grad, gain_grad, offset_grad, scale_grad, table_grad
        ):
            ref[...] = jnp.zeros_like(ref)
        roll_to_windows(
            lambda row: grad_first[row * SIDE : (row + 1) * SIDE, :],
            doubled, windows, shift_row, shift_col,
        )

    mine = pl.ds(pl.multiple_of(window * AREA, 16), AREA)
    z = windows[mine, :]
    n = n_in[...].astype(F32)
    gain_grad[...] += col_sum(z * n)
    offset_grad[...] += col_sum(z)
    grad_branch = norm_back(gain[0:1, :] * z, n, rstd_in[...])
    grad_low = grad_branch.astype(BF16)
    out_bias_grad[...] += col_sum(grad_branch)
    out_grad[...] += dot(mixture[0], grad_low, 1, 0)
    for head in range(HEADS):
        at = head * HEAD
        grad_mix = dot(out_weight[at : at + HEAD, :], grad_low, 1, 1)
        grad_mix = grad_mix.astype(BF16)
        low = probs[0, head]
        query = joint[0, at : at + HEAD, :]
        key = joint[0, D + at : D + at + HEAD, :]
        value = joint[0, 2 * D + at : 2 * D + at + HEAD, :]
        weight = low.astype(F32)
        weighted = weight * dot(value, grad_mix, 0, 0)
        grad_scores = weighted - weight * (col_sum(weighted) / col_sum(weight))
        table_grad[head] += grad_scores
        grad_raw = (grad_scores * scale[0, head]).astype(BF16)
        grad_query = dot(key, grad_raw, 1, 0)
        grad_key = dot(query, grad_raw, 1, 1)
        grad_value = dot(grad_mix, low, 1, 1)
        query = query.astype(F32)
        key = key.astype(F32)
        query_inner = col_sum(query * grad_query)
        key_inner = col_sum(key * grad_key)
        scale_grad[head : head + 1, :] += query_inner
        grad_query = inverse[0, head : head + 1, :] * (grad_query - query * query_inner)
        grad_key = inverse[0, HEADS + head : HEADS + head + 1, :] * (grad_key - key * key_inner)
        joint_grad[at : at + HEAD, :] = grad_query.astype(BF16)
        joint_grad[D + at : D + at + HEAD, :] = grad_key.astype(BF16)
        joint_grad[2 * D + at : 2 * D + at + HEAD, :] = grad_value.astype(BF16)
    in_grad[...] += dot(win_t[0], joint_grad[...], 1, 1)
    windows[mine, :] = dot(joint_grad[...], in_weight[...], 0, 1)

    @pl.when(window == WINDOWS - 1)
    def _():
        def write_row(row, line):
            tokens_grad[row] = line + grad_first[row * SIDE : (row + 1) * SIDE, :]

        roll_to_image(windows, doubled, write_row, shift_row, shift_col)


def attend_back(
    shifts, scale, grad_first, n, rstd, joint, probs, mixture, win_t, inverse,
    in_weight, out_weight, gain,
):
    per_window = lambda *dims: pl.BlockSpec((1,) + dims, lambda w: (w,) + (0,) * len(dims))
    rows = lambda width: pl.BlockSpec((AREA, width), lambda w: (w, 0))
    return pl.pallas_call(
        attend_back_kernel,
        grid=(WINDOWS,),
        in_specs=[
            smem(),
            smem(),
            whole((TOKENS, D)),
            rows(D),
            rows(1),
            per_window(3 * D, AREA),
            per_window(HEADS, AREA, AREA),
            per_window(D, AREA),
            per_window(D + 16, AREA),
            per_window(2 * HEADS, AREA),
            whole((D, 3 * D)),
            whole((D, D)),
            whole((3, D)),
        ],
        out_specs=(
            whole((SIDE, SIDE, D)),
            whole((D + 16, 3 * D)),
            whole((D, D)),
            whole((1, D)),
            whole((1, D)),
            whole((1, D)),
            whole((HEADS, AREA)),
            whole((HEADS, AREA, AREA)),
        ),
        out_shape=(
            full((SIDE, SIDE, D)),
            full((D + 16, 3 * D)),
            full((D, D)),
            full((1, D)),
            full((1, D)),
            full((1, D)),
            full((HEADS, AREA)),
            full((HEADS, AREA, AREA)),
        ),
        scratch_shapes=[
            pltpu.VMEM((SIDE, SIDE + WS, D), F32),
            pltpu.VMEM((TOKENS, D), F32),
            pltpu.VMEM((3 * D, AREA), BF16),
        ],
        compiler_params=params(),
        name="attend_back",
    )(
        shifts, scale, grad_first, n, rstd, joint, probs, mixture, win_t, inverse,
        in_weight, out_weight, gain,
    )


def table_back_kernel(table_grad, scale_rows, w1, b1, w2, out1, out2, out3, values_grad):
    spread = spread_matrix(True)
    for head in range(HEADS):
        high, low = split(table_grad[head])
        spread_low = spread.astype(BF16)
        flat = dot(high, spread_low, 1, 1) + dot(low, spread_low, 1, 1)
        flat = jnp.concatenate([flat, jnp.zeros((AREA, TABLE - 384), F32)], axis=1)
        total = jnp.zeros((16, TABLE), F32)
        for key_row in range(WS):
            shift = EXTENT * key_row
            line = flat[key_row * WS : (key_row + 1) * WS, :]
            line = jnp.concatenate([line, jnp.zeros((16 - WS, TABLE), F32)], axis=0)
            total += pltpu.roll(line, shift, 1)
        total = pltpu.roll(total, 0, 1, stride=1, stride_axis=0)
        values_grad[head : head + 1, :] = col_sum(total)
    f_row, f_col = offsets_row((UNITS, TABLE), 1, -1.0)
    w1t = jnp.transpose(w1[...], (1, 0))
    b1t = jnp.transpose(b1[...], (1, 0))
    hidden, slope = gelu_pair(w1t[:, 0:1] * f_row + w1t[:, 1:2] * f_col + b1t[:, 0:1])
    chance = jax.nn.sigmoid(exact_dot(w2[...], hidden, 0, 0))
    grad_pre = values_grad[:HEADS, :] * (16.0 * chance * (1.0 - chance))
    out2[...] = exact_dot(hidden, grad_pre, 1, 1)
    grad_hidden = exact_dot(w2[...], grad_pre, 1, 0) * slope
    f_row, f_col = offsets_row((8, TABLE), 1, -1.0)
    kind = iota((8, TABLE), 0)
    factors = jnp.where(kind == 0, f_row, jnp.where(kind == 1, f_col, 1.0))
    out1[...] = exact_dot(factors, grad_hidden, 1, 1)
    out3[...] = jnp.sum(scale_rows[...], axis=1, keepdims=True)


def table_back(table_grad, scale_rows, w1, b1, w2):
    return pl.pallas_call(
        table_back_kernel,
        out_shape=(full((8, UNITS)), full((UNITS, HEADS)), full((HEADS, 1))),
        scratch_shapes=[pltpu.VMEM((16, TABLE), F32)],
        compiler_params=params(),
        name="table_back",
    )(table_grad, scale_rows, w1, b1, w2)


def per_device(
    tokens, shifts, routes, cotangent, in_weight, in_bias, logit_scale,
    bias_net_first_weight, bias_net_first_bias, bias_net_second_weight,
    out_weight, out_bias, up_weight, up_bias, down_weight, down_bias, router_weight,
    expert_up, expert_up_bias, expert_down, expert_down_bias, norm_gain, norm_bias,
):
    experts = router_weight.shape[1]
    capacity = (5 * TOKENS + 4 * experts - 1) // (4 * experts)
    slots = -(-capacity // 16) * 16
    picture = tokens.reshape(SIDE, SIDE, D)
    cot = cotangent.reshape(SIDE, SIDE, D)
    route_col = routes.reshape(TOKENS, 1)
    first_bias = bias_net_first_bias.reshape(1, UNITS)

    slot_col, slot_row, cot_slots, table, scale = prep(
        route_col, cot, bias_net_first_weight, first_bias, bias_net_second_weight,
        logit_scale.reshape(1, HEADS), experts, capacity, slots,
    )
    exchange = lambda blocks: lax.all_to_all(
        blocks, "expert", split_axis=0, concat_axis=0, tiled=True
    )
    cot_arrived = exchange(cot_slots)
    normed, n_zero, rstd_zero, joint, probs, mixture, win_t, inverse = attend(
        shifts, scale, picture, in_weight, in_bias, table,
        out_weight, out_bias.reshape(1, D), norm_gain, norm_bias,
    )
    first_low, active, slope, n_one, rstd_one, second, buffer = forward(
        shifts, picture, normed, up_weight, up_bias.reshape(1, FF), down_weight,
        down_bias.reshape(1, D), norm_gain, norm_bias, slot_row, experts, slots,
    )
    arrived = exchange(buffer)
    (
        produced, grad_arrived, expert_up_grad, expert_up_bias_grad, expert_down_grad_t,
        expert_down_bias_grad,
    ) = run_experts(
        arrived, cot_arrived, router_weight, expert_up[0], expert_up_bias, expert_down[0],
        expert_down_bias, norm_gain,
    )
    returned = exchange(produced).reshape(-1, D)
    grad_returned = exchange(grad_arrived).reshape(-1, D)
    (
        result, grad_first, up_grad, up_bias_grad, down_grad_t, down_bias_grad, router_grad,
        gain_grad, offset_grad,
    ) = backward(
        second, cot, slot_col, route_col, returned, grad_returned, router_weight, first_low,
        active, slope, n_one, rstd_one, up_weight, down_weight, norm_gain, norm_bias,
    )
    (
        tokens_grad, in_grad, out_grad, out_bias_grad, gain_zero, offset_zero, scale_rows,
        table_grad,
    ) = attend_back(
        shifts, scale, grad_first, n_zero, rstd_zero, joint, probs, mixture, win_t, inverse,
        in_weight, out_weight, norm_gain,
    )
    table_one, table_two, scale_grad = table_back(
        table_grad, scale_rows, bias_net_first_weight, first_bias, bias_net_second_weight
    )

    low_sum = lambda parts, axes: [
        part.astype(F32)
        for part in lax.psum([part.astype(BF16) for part in parts], axes)
    ]
    expert_up_grad, expert_down_grad_t, expert_up_bias_grad, expert_down_bias_grad = low_sum(
        [expert_up_grad, expert_down_grad_t, expert_up_bias_grad, expert_down_bias_grad], "dp"
    )
    both = ("dp", "expert")
    up_grad, down_grad_t = low_sum([up_grad, down_grad_t], both)
    in_weight_grad, out_grad = low_sum([in_grad[:D], out_grad], both)
    smalls = [
        in_grad[D], out_bias_grad, up_bias_grad, down_bias_grad, router_grad,
        gain_zero, gain_grad[1:], offset_zero, offset_grad[1:],
        table_one[:3], table_two, scale_grad,
    ]
    sizes = [small.size for small in smalls]
    packed = lax.psum(jnp.concatenate([small.reshape(-1) for small in smalls]), both)
    pieces = []
    at = 0
    for size in sizes:
        pieces.append(packed[at : at + size])
        at += size
    (
        in_bias_all, out_bias_grad, up_bias_grad, down_bias_grad, router_grad,
        gain_zero, gain_rest, offset_zero, offset_rest, table_one, table_two, scale_grad,
    ) = pieces
    return (
        result.reshape(tokens.shape),
        tokens_grad.reshape(tokens.shape),
        in_weight_grad,
        jnp.stack([in_bias_all[:D], in_bias_all[2 * D :]]),
        scale_grad,
        table_one[: 2 * UNITS].reshape(2, UNITS),
        table_one[2 * UNITS :],
        table_two.reshape(UNITS, HEADS),
        out_grad,
        out_bias_grad,
        up_grad,
        up_bias_grad,
        down_grad_t.T,
        down_bias_grad,
        router_grad.reshape(D, experts),
        expert_up_grad[None],
        expert_up_bias_grad,
        expert_down_grad_t.T[None],
        expert_down_bias_grad,
        jnp.concatenate([gain_zero, gain_rest]).reshape(3, D),
        jnp.concatenate([offset_zero, offset_rest]).reshape(3, D),
    )


def solution(mesh):
    split_all = P(("dp", "expert"))
    placed = (split_all,) * 4 + (P(),) * 13 + (P("expert"),) * 4 + (P(),) * 2
    return jax.shard_map(
        per_device,
        mesh=mesh,
        in_specs=placed,
        out_specs=(split_all,) * 2 + (P(),) * 13 + (P("expert"),) * 4 + (P(),) * 2,
        check_vma=False,
    )
```

time: 895 us -> 490 us (0.55)
  the two profiles are of different devices: /device:TPU:25 before, /device:TPU:0 now
where the time goes in v1:
time: 490 us; the launch traced here: 484 us
  Pallas kernels  217 us (44%)
  waiting for transfers between devices  99.6 us (20%)
  blocking collectives  97.4 us (20%)
  local copies, waits for them, and re-layouts  29.3 us (6%)
  other arithmetic  18.2 us (4%)
  between operations  14.7 us (3%)
  starting transfers between devices  7.54 us (2%)
    psum x2, waiting for transfers between devices, per_device(): lax.psum([part.astype(BF16) for part in parts], axes)  84.9 us
    pallas_call x1, Pallas kernels, attend_back(): pl.pallas_call(attend_back_kernel, grid=(WINDOWS,), in_specs=[smem(), sme...  63.3 us
    pallas_call x1, Pallas kernels, attend(): pl.pallas_call(attend_kernel, grid=(WINDOWS,), in_specs=[smem(), smem(),...  59 us
    all_to_all x2, blocking collectives, per_device(): lax.all_to_all(blocks, 'expert', split_axis=0, concat_axis=0, tiled=True)  43.1 us
    psum x1, blocking collectives, per_device(): lax.psum(jnp.concatenate([small.reshape(-1) for small in smalls]), both)  39.2 us
    pallas_call x1, Pallas kernels, run_experts(): pl.pallas_call(expert_kernel, grid=(sources,), in_specs=[block, block, wh...  29 us
    pallas_call x1, Pallas kernels, backward(): pl.pallas_call(backward_kernel, grid=(TOKENS // ROWS,), in_specs=[rows(D)...  28.7 us
    pallas_call x1, Pallas kernels, forward(): pl.pallas_call(forward_kernel, grid=(TOKENS // ROWS,), in_specs=[smem(),...  19.1 us
  transfers between devices with their start and end apart: 4, of which 2 were waited for; matrix products, arithmetic and copies ran while one was open for 6% of the time, Pallas kernels for 21%

profile of v1, /device:TPU:0, one launch (start us, length us, event | category | flops | bytes accessed | tf_op | source)
XLA Modules:
  0.0 483.8 jit_solution(2421570677733330362)
XLA Ops:
  7.2 1.8 copy.51.routes
  9.0 1.6 copy.52.w2
  10.6 1.2 reshape.147.out_bias
  11.9 1.3 reshape.148.up_bias
  13.2 1.2 reshape.149.down_bias
  14.4 9.5 %prep.1 = (s32[1296,1]{1,0:T(8,128)}, s32[1,1296]{1,0:T(1,128)}, bf16[4,416,384]{2,1,0:T(8,128)(2,1)}, f32[12,144,144]{2,1,0:T(8,128)}, f32[1,12]{1,0:T(1,128)}) custom-call(s32[1296,1]{1,0:T(8,128)} %copy.51.routes, bf16[36,36,384]{2,1,0:T(8,128)(2,1)} %bitcast.21, f32[2,512]{1,0:T(2,128)} %w1.3, f32[1,512]{1,0:T(1,128)} %bitcast.28, f32[512,12]{1,0:T(8,128)} %copy.52.w2, ...), custom_call_target="tpu_custom_call" | custom-call | tf_op jit(solution)/shard_map/prep/pallas_call | solution.py:175
  23.9 59.0 %attend.1 = (f32[1296,384]{1,0:T(8,128)}, bf16[1296,384]{1,0:T(8,128)(2,1)}, f32[1296,1]{1,0:T(8,128)}, bf16[9,1152,144]{2,1,0:T(8,128)(2,1)}, bf16[9,12,144,144...) custom-call(s32[1,2]{1,0:T(1,128)} %shifts.5, ...), custom_call_target="tpu_custom_call" | custom-call | tf_op jit(solution)/shard_map/attend/pallas_call | solution.py:287
  82.9 19.1 %forward.1 = (bf16[1296,384]{1,0:T(8,128)(2,1)}, bf16[1296,1536]{1,0:T(8,128)(2,1)}, bf16[1296,1536]{1,0:T(8,128)(2,1)}, bf16[1296,384]{1,0:T(8,128)(2,1)}, f32[...) custom-call(s32[1,2]{1,0:T(1,128)} %shifts.5, bf16[36,36,384]{2,1,0:T(8,128)(2,1)} %bitcast.24, ...), custom_call_target="tpu_custom_call" | custom-call | tf_op jit(solution)/shard_map/forward/pallas_call | solution.py:378
  102.0 22.6 %all_to_all.20.arrived = bf16[4,416,384]{2,1,0:T(8,128)(2,1)} all-to-all(bf16[4,416,384]{2,1,0:T(8,128)(2,1)} %get-tuple-element.73), channel_id=1, replica_groups=mesh['dp'=8,'expert'=4] {'expert'}, dimensions={0} | all-to-all | bytes 2555904 | tf_op jit(solution)/shard_map/all_to_all | solution.py:817
  124.6 3.9 all-to-all-start.1
  128.5 0.8 copy.53.router
  129.3 14.7 %all-to-all-done.1.cot = bf16[4,416,384]{2,1,0:T(8,128)(2,1)S(1)} async-done(((bf16[4,416,384]{2,1,0:T(8,128)(2,1)}), bf16[4,416,384]{2,1,0:T(8,128)(2,1)S(1)}, u32[]{:S(2)}, u32[]{:S(2)}) %all-to-all-start.1) | async-done | bytes 1277984 | tf_op jit(solution)/shard_map/all_to_all | solution.py:817
  144.0 1.0 copy-done.1
  145.1 29.0 %experts.1 = (bf16[4,416,384]{2,1,0:T(8,128)(2,1)}, bf16[4,416,384]{2,1,0:T(8,128)(2,1)}, f32[384,1536]{1,0:T(8,128)}, f32[1,1536]{1,0:T(1,128)}, f32[384,1536]{1,0:T(8,128)}, /*index=5*/f32[1,384]{1,0:T(1,128)}) custom-call(bf16[4,416,384]{2,1,0:T(8,128)(2,1)} %all_to_all.20.arrived, bf16[4,416,384]{2,1,0:T(8,128)(2,1)} %copy-done.1, ...), custom_call_target="tpu_custom_call" | custom-call | tf_op jit(solution)/shard_map/experts/pallas_call | solution.py:473
  174.1 20.5 %all_to_all.21 = bf16[4,416,384]{2,1,0:T(8,128)(2,1)} all-to-all(bf16[4,416,384]{2,1,0:T(8,128)(2,1)} %get-tuple-element.75), channel_id=1, replica_groups=mesh['dp'=8,'expert'=4] {'expert'}, dimensions={0} | all-to-all | bytes 2555904 | tf_op jit(solution)/shard_map/all_to_all | solution.py:817
  194.6 3.5 all-to-all-start.3
  198.2 4.2 convert_bitcast_fusion
  202.4 0.6 copy-done.12
  203.1 15.1 %all-reduce.1 = (bf16[1,1536]{1,0:T(2,128)(2,1)S(1)}, bf16[1,384]{1,0:T(2,128)(2,1)S(1)}) all-reduce(bf16[1,1536]{1,0:T(2,128)(2,1)S(1)} %convert_element_type.47, bf16[1,384]{1,0:T(2,128)(2,1)S(1)} %convert_element_type.50), channel_id=1, replica_groups=mesh['dp'=8,'expert'=4] {'dp'}, use_global_device_ids=true, to_apply=%region_6.0 | all-reduce | flops 1920 | bytes 7680 | tf_op jit(solution)/shard_map/psum | solution.py:859
  218.1 0.6 convert_element_type.48
  219.3 1.0 copy-done
  220.3 28.7 %backward.1 = (bf16[36,36,384]{2,1,0:T(8,128)(2,1)}, f32[1296,384]{1,0:T(8,128)}, f32[384,1536]{1,0:T(8,128)}, f32[1,1536]{1,0:T(1,128)}, f32[384,1536]{1,0:T(8,...) custom-call(f32[1296,384]{1,0:T(8,128)} %get-tuple-element.71.second, ...), custom_call_target="tpu_custom_call" | custom-call | tf_op jit(solution)/shard_map/backward/pallas_call | solution.py:584
  249.1 63.3 %attend_back.1 = (f32[36,36,384]{2,1,0:T(8,128)}, f32[400,1152]{1,0:T(8,128)}, f32[384,384]{1,0:T(8,128)}, f32[1,384]{1,0:T(1,128)}, f32[1,384]{1,0:T(1,128)}, /...) custom-call(s32[1,2]{1,0:T(1,128)} %shifts.5, f32[1,12]{1,0:T(1,128)} %get-tuple-element.67.scale, ...), custom_call_target="tpu_custom_call" | custom-call | tf_op jit(solution)/shard_map/attend_back/pallas_call | solution.py:708
  312.4 8.6 %table_back.1 = (f32[8,512]{1,0:T(8,128)}, f32[512,12]{1,0:T(8,128)}, f32[12,1]{1,0:T(8,128)}) custom-call(f32[12,144,144]{2,1,0:T(8,128)} %get-tuple-element.101.table_grad, f32[12,144]{1,0:T(8,128)} %get-tuple-element.102.scale_rows, f32[2,512]{1,0:T(2,128)} %w1.3, f32[1,512]{1,0:T(1,128)} %bitcast.29, f32[512,12]{1,0:T(8,128)} %copy.52.w2), custom_call_target="tpu_custom_call" | custom-call | tf_op jit(solution)/shard_map/table_back/pallas_call | solution.py:790
  321.0 0.9 slice.78
  322.3 1.1 reshape.163
  323.4 0.8 reduce.6
  324.2 2.5 slice.102
  326.7 0.7 convert_element_type.41
  327.5 1.1 convert_element_type.43
  328.6 0.8 slice_reduce_fusion
  329.5 1.1 convert_bitcast_fusion.2
  330.8 39.2 %psum.64 = f32[14988]{0:T(1024)S(1)} all-reduce(f32[14988]{0:T(1024)S(1)} %constant_dynamic-update-slice_fusion), channel_id=1, replica_groups=mesh['dp'=8,'expert'=4] {'dp','expert'}, use_global_device_ids=true, to_apply=%region_1.0 | all-reduce | flops 14988 | bytes 119904 | tf_op jit(solution)/shard_map/psum | solution.py:873
  371.5 0.7 copy.58
  372.2 0.6 fusion.1
  373.0 0.7 copy.60
  373.7 0.6 reshape.168
  374.3 0.6 reshape.169
  375.5 0.6 reshape.165
  376.1 3.3 copy.57
  379.4 0.6 pad_maximum_fusion
  380.0 3.1 broadcast_in_dim.13
  383.1 1.7 copy.61
  384.8 84.9 %all-reduce.6.cloned.1.call-done = (bf16[1536,384]{0,1:T(8,128)(2,1)}, bf16[384,1152]{1,0:T(8,128)(2,1)}, bf16[384,384]{1,0:T(8,128)(2,1)}, bf16[384,1536]{1,0:T(8,128)(2,1)}) async-done(((bf16[1536,384]{0,1:T(8,128)(2,1)}, bf16[384,1152]{1,0:T(8,128)(2,1)}, bf16[384,384]{1,0:T(8,128)(2,1)}, bf16[384,1536]{1,0:T(8,128)(2,1)}), (bf16[1536,384]{0,1:T(8,128)(2,1)}, bf16[384,1152]{1,0:T(8,128)(2,1)}, ...) | async-done | bytes 3538960 | tf_op jit(solution)/shard_map/psum | solution.py:859
  469.7 3.1 convert_element_type.44
  472.8 1.7 copy.59
  474.5 1.3 convert_element_type.40
  475.8 0.9 convert_element_type.42
  (82 shorter events, 3.4 us)
Async XLA Ops:
  124.6 3.9 copy-start.11
  124.6 19.4 %all-to-all-start.1 = ((bf16[4,416,384]{2,1,0:T(8,128)(2,1)}), bf16[4,416,384]{2,1,0:T(8,128)(2,1)S(1)}, u32[]{:S(2)}, u32[]{:S(2)}) async-start(bf16[4,416,384]{2,1,0:T(8,128)(2,1)} %get-tuple-element.74), calls=%async_computation.1 | async-start | bytes 2555904 | tf_op jit(solution)/shard_map/all_to_all | solution.py:817
  144.0 1.0 copy-start.1
  194.6 24.7 %all-to-all-start.3 = ((bf16[4,416,384]{2,1,0:T(8,128)(2,1)}), bf16[4,416,384]{2,1,0:T(8,128)(2,1)S(1)}, u32[]{:S(2)}, u32[]{:S(2)}) async-start(bf16[4,416,384]{2,1,0:T(8,128)(2,1)} %get-tuple-element.76), calls=%async_computation.3 | async-start | bytes 2555904 | tf_op jit(solution)/shard_map/all_to_all | solution.py:817
  198.1 181.9 %all-reduce.8.cloned.1.call-start = ((), (), s32[]{:S(2)}) async-start(), calls=%async_computation.5 | async-start | bytes 4718592 | tf_op jit(solution)/shard_map/psum | solution.py:859
  202.4 0.7 copy-start.12
  202.4 0.7 copy-start.16
  202.4 267.3 %all-reduce.6.cloned.1.call-start = ((), (), s32[]{:S(2)}) async-start(), calls=%async_computation.4 | async-start | bytes 7077888 | tf_op jit(solution)/shard_map/psum | solution.py:859
  219.3 1.0 copy-start
  312.3 9.6 %copy-start.20 = (f32[1,384]{1,0:T(1,128)S(1)}, f32[1,384]{1,0:T(1,128)}, u32[]{:S(2)}) copy-start(f32[1,384]{1,0:T(1,128)} %get-tuple-element.93) | copy-start | bytes 4612
  312.4 9.6 %copy-start.13 = (f32[1,1536]{1,0:T(1,128)S(1)}, f32[1,1536]{1,0:T(1,128)}, u32[]{:S(2)}) copy-start(f32[1,1536]{1,0:T(1,128)} %get-tuple-element.94) | copy-start | bytes 18436
  312.4 9.6 %copy-start.17 = (f32[1,384]{1,0:T(1,128)S(1)}, f32[1,384]{1,0:T(1,128)}, u32[]{:S(2)}) copy-start(f32[1,384]{1,0:T(1,128)} %get-tuple-element.95) | copy-start | bytes 4612
  312.4 9.6 %copy-start.10 = (f32[384,4]{1,0:T(8,128)S(1)}, f32[384,4]{1,0:T(8,128)}, u32[]{:S(2)}) copy-start(f32[384,4]{1,0:T(8,128)} %get-tuple-element.96) | copy-start | bytes 18436
  312.4 9.8 %copy-start.19 = (f32[1,384]{1,0:T(1,128)S(1)}, f32[1,384]{1,0:T(1,128)}, u32[]{:S(2)}) copy-start(f32[1,384]{1,0:T(1,128)} %get-tuple-element.97) | copy-start | bytes 4612
  312.4 9.8 %copy-start.15 = (f32[3,384]{1,0:T(4,128)S(1)}, f32[3,384]{1,0:T(4,128)}, u32[]{:S(2)}) copy-start(f32[3,384]{1,0:T(4,128)} %get-tuple-element.98) | copy-start | bytes 13828
  312.4 9.8 %copy-start.18 = (f32[1,384]{1,0:T(1,128)S(1)}, f32[1,384]{1,0:T(1,128)}, u32[]{:S(2)}) copy-start(f32[1,384]{1,0:T(1,128)} %get-tuple-element.99) | copy-start | bytes 4612
  312.4 9.8 %copy-start.14 = (f32[3,384]{1,0:T(4,128)S(1)}, f32[3,384]{1,0:T(4,128)}, u32[]{:S(2)}) copy-start(f32[3,384]{1,0:T(4,128)} %get-tuple-element.100) | copy-start | bytes 13828
  312.4 14.3 %copy-start.8 = (f32[384,384]{1,0:T(8,128)S(1)}, f32[384,384]{1,0:T(8,128)}, u32[]{:S(2)}) copy-start(f32[384,384]{1,0:T(8,128)} %get-tuple-element.106) | copy-start | bytes 1769476
  321.0 6.4 %copy-start.3 = (f32[384,1536]{1,0:T(8,128)S(1)}, f32[384,1536]{1,0:T(8,128)}, u32[]{:S(2)}) copy-start(f32[384,1536]{1,0:T(8,128)} %get-tuple-element.107) | copy-start | bytes 7077892
  327.4 2.1 copy-start.2
  330.7 45.4 %copy-start.4 = (f32[36,36,384]{2,1,0:T(8,128)S(1)}, f32[36,36,384]{2,1,0:T(8,128)}, u32[]{:S(2)}) copy-start(f32[36,36,384]{2,1,0:T(8,128)} %get-tuple-element.91) | copy-start | bytes 5971972
  380.0 3.1 copy-start.5
  469.7 3.1 copy-start.6
  472.8 1.7 copy-start.7
  474.5 1.3 copy-start.9
Sparse Core Ops, SparseCore 0:
  202.5 68.4 all-reduce.7
  330.8 138.8 all-reduce.5

commit v2 on v1

--- a/solution.py
+++ b/solution.py
@@ -104,6 +104,154 @@
     return pltpu.CompilerParams(vmem_limit_bytes=VMEM_LIMIT, **more)
 
 
+def partner(me, step, count):
+    side = 1
+    while side * side < count:
+        side *= 2
+    if side * side != count:
+        return lax.rem(me + step, count)
+    row = lax.rem(lax.div(me, side) + step // side, side)
+    col = lax.rem(lax.rem(me, side) + step % side, side)
+    return row * side + col
+
+
+def opposite(step, count):
+    side = 1
+    while side * side < count:
+        side *= 2
+    if side * side != count:
+        return (count - step) % count
+    return ((side - step // side) % side) * side + (side - step % side) % side
+
+
+def greet(devices):
+    barrier = pltpu.get_barrier_semaphore()
+    for device in devices:
+        pl.semaphore_signal(barrier, inc=1, device_id=device, device_id_type=pl.DeviceIdType.MESH)
+    pl.semaphore_wait(barrier, len(devices))
+
+
+def levels_of(names):
+    dp = lax.axis_index("dp")
+    depth = lax.axis_size("dp") // 2
+    core = lax.rem(dp, 2)
+    place = lax.div(dp, 2)
+    levels = [(2, core, lambda j: {"dp": place * 2 + j})]
+    if "expert" in names:
+        levels.append((lax.axis_size("expert"), lax.axis_index("expert"), lambda j: {"expert": j}))
+    if depth > 1:
+        levels.append((depth, place, lambda j: {"dp": j * 2 + core}))
+    return levels
+
+
+def level_counts(names, dp, experts):
+    counts = [2] + ([experts] if "expert" in names else []) + ([dp // 2] if dp > 2 else [])
+    return counts
+
+
+def padded_rows(rows, counts, tile):
+    unit = tile
+    for count in counts:
+        unit *= count
+    return -(-rows // unit) * unit
+
+
+def land_shapes(rows, width, dtype, counts):
+    shapes = []
+    for count in counts:
+        rows //= count
+        shapes.append(pltpu.VMEM((count - 1, rows, width), dtype))
+    return shapes
+
+
+def sum_sems(counts):
+    return [pltpu.SemaphoreType.DMA((2 * len(counts), max(counts)))] * 2
+
+
+class Sum:
+    def __init__(self, source, held, result, lands, send, recv, levels):
+        self.source, self.held, self.result, self.lands = source, held, result, lands
+        self.send, self.recv, self.levels = send, recv, levels
+        rows = source.shape[0]
+        start = 0
+        self.regions = []
+        for count, index, _ in levels:
+            rows //= count
+            self.regions.append((start, rows))
+            start = start + index * rows
+
+    def scatter(self, level, begin):
+        count, index, device = self.levels[level]
+        start, rows = self.regions[level]
+        ref = self.held if level else self.source
+        into = self.held if level < len(self.levels) - 1 else self.result
+        for step in range(1, count):
+            to = lax.rem(index + step, count)
+            copy = pltpu.make_async_remote_copy(
+                src_ref=ref.at[pl.ds(pl.multiple_of(start + to * rows, 8), rows)],
+                dst_ref=self.lands[level].at[step - 1],
+                send_sem=self.send.at[level, step],
+                recv_sem=self.recv.at[level, step],
+                device_id=device(to),
+                device_id_type=pl.DeviceIdType.MESH,
+            )
+            copy.start() if begin else copy.wait()
+        if begin:
+            return
+        mine = start + index * rows
+        tile = 16 if ref.dtype == BF16 else 8
+        chunk = tile
+        while rows % (chunk * 2) == 0 and chunk < 128:
+            chunk *= 2
+
+        def add(i, carry):
+            here = pl.ds(pl.multiple_of(mine + i * chunk, tile), chunk)
+            there = pl.ds(pl.multiple_of(i * chunk, tile), chunk)
+            total = ref[here, :].astype(F32)
+            for step in range(1, count):
+                total = total + self.lands[level][step - 1, there, :].astype(F32)
+            into[here, :] = total.astype(into.dtype)
+            return carry
+
+        lax.fori_loop(0, rows // chunk, add, 0)
+
+    def gather(self, level, begin):
+        count, index, device = self.levels[level]
+        start, rows = self.regions[level]
+        mine = self.result.at[pl.ds(pl.multiple_of(start + index * rows, 8), rows)]
+        for step in range(1, count):
+            to = lax.rem(index + step, count)
+            copy = pltpu.make_async_remote_copy(
+                src_ref=mine,
+                dst_ref=mine,
+                send_sem=self.send.at[len(self.levels) + level, step],
+                recv_sem=self.recv.at[len(self.levels) + level, step],
+                device_id=device(to),
+                device_id_type=pl.DeviceIdType.MESH,
+            )
+            copy.start() if begin else copy.wait()
+
+    def stages(self):
+        last = len(self.levels) - 1
+        moves = [(self.scatter, level) for level in range(last + 1)]
+        moves += [(self.gather, level) for level in range(last, -1, -1)]
+
+        def stage(k):
+            if k:
+                moves[k - 1][0](moves[k - 1][1], False)
+            if k < len(moves):
+                moves[k][0](moves[k][1], True)
+
+        return [functools.partial(stage, k) for k in range(len(moves) + 1)]
+
+
+def greeted(levels):
+    devices = []
+    for count, index, device in levels:
+        devices += [device(lax.rem(index + step, count)) for step in range(1, count)]
+    return devices
+
+
 def offsets_row(shape, dim, sign):
     place = iota(shape, dim)
     row = jnp.floor((place.astype(F32) + 0.5) * (1.0 / EXTENT)).astype(I32)
@@ -232,15 +380,34 @@
 
 
 def attend_kernel(
-    shifts, scale, tokens, in_weight, in_bias, table, out_weight, out_bias, gain, offset,
-    normed, n_out, rstd_out, joint, probs, mixture, win_t, inverse,
-    doubled, windows, in_weight_t, bias_col,
+    cot_slots, shifts, scale, tokens, in_weight, in_bias, table, out_weight, out_bias, gain, offset,
+    cot_arrived, normed, n_out, rstd_out, joint, probs, mixture, win_t, inverse,
+    doubled, windows, in_weight_t, bias_col, send, recv, local,
 ):
     window = pl.program_id(0)
     shift_row, shift_col = shifts[0, 0], shifts[0, 1]
+    me = lax.axis_index("expert")
+    count = cot_slots.shape[0]
+
+    def move(step):
+        to = partner(me, step, count)
+        return pltpu.make_async_remote_copy(
+            src_ref=cot_slots.at[to],
+            dst_ref=cot_arrived.at[me],
+            send_sem=send.at[step],
+            recv_sem=recv.at[step],
+            device_id={"expert": to},
+            device_id_type=pl.DeviceIdType.MESH,
+        )
+
+    keep = pltpu.make_async_copy(cot_slots.at[me], cot_arrived.at[me], local)
 
     @pl.when(window == 0)
     def _():
+        greet([{"expert": partner(me, step, count)} for step in range(1, count)])
+        for step in range(1, count):
+            move(step).start()
+        keep.start()
         roll_to_windows(
             lambda row: tokens[row].astype(F32), doubled, windows, shift_row, shift_col
         )
@@ -280,14 +447,23 @@
     n_out[...] = n.astype(BF16)
     rstd_out[...] = rstd
 
-
-def attend(shifts, scale, tokens, in_weight, in_bias, table, out_weight, out_bias, gain, offset):
+    @pl.when(window == WINDOWS - 1)
+    def _():
+        for step in range(1, count):
+            move(step).wait()
+        keep.wait()
+
+
+def attend(
+    cot_slots, shifts, scale, tokens, in_weight, in_bias, table, out_weight, out_bias, gain, offset
+):
     per_window = lambda *dims: pl.BlockSpec((1,) + dims, lambda w: (w,) + (0,) * len(dims))
     rows = lambda width: pl.BlockSpec((AREA, width), lambda w: (w, 0))
     return pl.pallas_call(
         attend_kernel,
         grid=(WINDOWS,),
         in_specs=[
+            pl.BlockSpec(memory_space=pl.ANY),
             smem(),
             smem(),
             whole((SIDE, SIDE, D)),
@@ -300,6 +476,7 @@
             whole((3, D)),
         ],
         out_specs=(
+            pl.BlockSpec(memory_space=pl.ANY),
             rows(D),
             rows(D),
             rows(1),
@@ -310,6 +487,7 @@
             per_window(2 * HEADS, AREA),
         ),
         out_shape=(
+            full(cot_slots.shape, BF16),
             full((TOKENS, D)),
             full((TOKENS, D), BF16),
             full((TOKENS, 1)),
@@ -324,10 +502,13 @@
             pltpu.VMEM((TOKENS, D), F32),
             pltpu.VMEM((3 * D, D), BF16),
             pltpu.VMEM((D, 128), F32),
+            pltpu.SemaphoreType.DMA((cot_slots.shape[0],)),
+            pltpu.SemaphoreType.DMA((cot_slots.shape[0],)),
+            pltpu.SemaphoreType.DMA(()),
         ],
-        compiler_params=params(),
+        compiler_params=params(collective_id=0, has_side_effects=True),
         name="attend",
-    )(shifts, scale, tokens, in_weight, in_bias, table, out_weight, out_bias, gain, offset)
+    )(cot_slots, shifts, scale, tokens, in_weight, in_bias, table, out_weight, out_bias, gain, offset)
 
 
 def forward_kernel(
@@ -419,102 +600,153 @@
 
 
 def expert_kernel(
-    arrived, cot, router, up, up_bias, down, down_bias, gain,
-    out, grad_in, up_grad, up_bias_grad, down_grad_t, down_bias_grad,
-    active, slope, grad_hidden_sum,
+    buffer, cot, router, up, up_bias, down, down_bias, gain,
+    out, grad_in, packed,
+    arrived, outs, grads, active, slope, up_grad, down_grad_t, up_bias_grad, down_bias_grad,
+    send, recv,
 ):
-    source = pl.program_id(0)
     me = lax.axis_index("expert")
-
-    @pl.when(source == 0)
-    def _():
-        for ref in (up_grad, up_bias_grad, down_grad_t, down_bias_grad):
-            ref[...] = jnp.zeros_like(ref)
-
-    features = arrived[0]
-    slots = features.shape[0]
+    count, slots, _ = buffer.shape
+    others = range(1, count)
+
+    def move(kind, step, source, target, to):
+        return pltpu.make_async_remote_copy(
+            src_ref=source,
+            dst_ref=target,
+            send_sem=send.at[kind, step],
+            recv_sem=recv.at[kind, step],
+            device_id={"expert": to},
+            device_id_type=pl.DeviceIdType.MESH,
+        )
+
+    greet([{"expert": partner(me, step, count)} for step in others])
+    for step in others:
+        to = partner(me, step, count)
+        move(0, step, buffer.at[to], arrived.at[step], to).start()
+    arrived[0] = buffer[me]
+    for ref in (up_grad, up_bias_grad, down_grad_t, down_bias_grad):
+        ref[...] = jnp.zeros_like(ref)
     router_high, router_low = split(router[...])
-    logits = dot(features, router_high, 1, 0) + dot(features, router_low, 1, 0)
-    chances = jnp.exp(logits - jnp.max(logits, axis=1, keepdims=True))
-    own = jnp.where(iota(chances.shape, 1) == me, chances, 0.0)
-    gate = jnp.sum(own, axis=1, keepdims=True) / jnp.sum(chances, axis=1, keepdims=True)
-
-    output = jnp.broadcast_to(down_bias[...], (slots, D))
-    for at in range(0, FF, CHUNK):
-        hidden = dot(features, up[:, at : at + CHUNK], 1, 0) + up_bias[:, at : at + CHUNK]
-        activated, derivative = gelu_pair(hidden)
-        activated = activated.astype(BF16)
-        active[:, at : at + CHUNK] = activated
-        slope[:, at : at + CHUNK] = derivative
-        output += dot(activated, down[at : at + CHUNK, :], 1, 0)
-    output = output.astype(BF16)
-    out[0] = output
-    n, rstd = norm_parts(gate * output.astype(F32))
-    grad_output = gate * norm_back(gain[2:3, :] * cot[0].astype(F32), n, rstd)
-    grad_low = grad_output.astype(BF16)
-    down_bias_grad[...] += col_sum(grad_low.astype(F32))
-    grad_low_t = jnp.transpose(grad_low, (1, 0))
-    features_t = jnp.transpose(features, (1, 0))
-    grad_features = jnp.zeros((slots, D), F32)
-    for at in range(0, FF, CHUNK):
-        part = slice(at, at + CHUNK)
-        grad_hidden = dot(grad_low, down[part, :], 1, 1) * slope[:, part]
-        grad_hidden_low = grad_hidden.astype(BF16)
-        up_bias_grad[:, part] += col_sum(grad_hidden)
-        down_grad_t[:, part] += dot(grad_low_t, active[:, part], 1, 0)
-        up_grad[:, part] += dot(features_t, grad_hidden_low, 1, 0)
-        grad_features += dot(grad_hidden_low, up[:, part], 1, 1)
-    grad_in[0] = grad_features.astype(BF16)
-
-
-def run_experts(arrived, cot, router, up, up_bias, down, down_bias, gain):
-    sources, slots, _ = arrived.shape
-    block = pl.BlockSpec((1, slots, D), lambda i: (i, 0, 0))
+
+    def work(step, carry):
+        if count == 4:
+            owner = lax.rem(lax.div(me, 2) + lax.div(step, 2), 2) * 2
+            owner = owner + lax.rem(lax.rem(me, 2) + lax.rem(step, 2), 2)
+        else:
+            side = 1
+            while side * side < count:
+                side *= 2
+            if side * side == count:
+                owner = lax.rem(lax.div(me, side) + side - lax.div(step, side), side) * side
+                owner = owner + lax.rem(lax.rem(me, side) + side - lax.rem(step, side), side)
+            else:
+                owner = lax.rem(me + count - step, count)
+
+        @pl.when(step > 0)
+        def _():
+            move(0, step, buffer.at[owner], arrived.at[step], owner).wait_recv()
+
+        features = arrived[step]
+        logits = dot(features, router_high, 1, 0) + dot(features, router_low, 1, 0)
+        chances = jnp.exp(logits - jnp.max(logits, axis=1, keepdims=True))
+        own = jnp.where(iota(chances.shape, 1) == me, chances, 0.0)
+        gate = jnp.sum(own, axis=1, keepdims=True) / jnp.sum(chances, axis=1, keepdims=True)
+
+        output = jnp.zeros((slots, D), F32)
+        for at in range(0, FF, CHUNK):
+            hidden = dot(features, up[:, at : at + CHUNK], 1, 0) + up_bias[:, at : at + CHUNK]
+            activated, derivative = gelu_pair(hidden)
+            activated = activated.astype(BF16)
+            active[:, at : at + CHUNK] = activated
+            slope[:, at : at + CHUNK] = derivative
+            output += dot(activated, down[at : at + CHUNK, :], 1, 0)
+        output = (output + down_bias[...]).astype(BF16)
+        outs[step] = output
+
+        @pl.when(step > 0)
+        def _():
+            move(1, step, outs.at[step], out.at[me], owner).start()
+
+        n, rstd = norm_parts(gate * output.astype(F32))
+        grad_output = gate * norm_back(gain[2:3, :] * cot[owner].astype(F32), n, rstd)
+        grad_low = grad_output.astype(BF16)
+        down_bias_grad[...] += col_sum(grad_low.astype(F32))
+        grad_low_t = jnp.transpose(grad_low, (1, 0))
+        features_t = jnp.transpose(features, (1, 0))
+        grad_features = jnp.zeros((slots, D), F32)
+        for at in range(0, FF, CHUNK):
+            part = slice(at, at + CHUNK)
+            grad_hidden = dot(grad_low, down[part, :], 1, 1) * slope[:, part]
+            grad_hidden_low = grad_hidden.astype(BF16)
+            up_bias_grad[:, part] += col_sum(grad_hidden)
+            down_grad_t[:, part] += dot(grad_low_t, active[:, part], 1, 0)
+            up_grad[:, part] += dot(features_t, grad_hidden_low, 1, 0)
+            grad_features += dot(grad_hidden_low, up[:, part], 1, 1)
+        grads[step] = grad_features.astype(BF16)
+
+        @pl.when(step > 0)
+        def _():
+            move(2, step, grads.at[step], grad_in.at[me], owner).start()
+
+        return carry
+
+    lax.fori_loop(0, count, work, 0)
+    out[me] = outs[0]
+    grad_in[me] = grads[0]
+    pack_pair(packed, up_grad, down_grad_t)
+    packed[2 * FF :, :] = jnp.zeros_like(packed[2 * FF :, :])
+    tail = jnp.concatenate(
+        [up_bias_grad[:, at : at + D] for at in range(0, FF, D)]
+        + [down_bias_grad[...], jnp.zeros((11, D), F32)],
+        axis=0,
+    )
+    packed[2 * FF : 2 * FF + 16, :] = tail.astype(BF16)
+    for step in others:
+        to = partner(me, step, count)
+        move(0, step, buffer.at[to], arrived.at[step], to).wait_send()
+        for kind, source, target in ((1, outs, out), (2, grads, grad_in)):
+            move(kind, step, source.at[step], target.at[me], to).wait()
+
+
+def pack_pair(packed, up_grad, down_grad_t):
+    for block in range(FF // D):
+        part = slice(block * D, (block + 1) * D)
+        packed[part, :] = up_grad[:, part].astype(BF16)
+        packed[FF + block * D : FF + (block + 1) * D, :] = jnp.transpose(
+            down_grad_t[:, part].astype(BF16), (1, 0)
+        )
+
+
+def run_experts(buffer, cot, router, up, up_bias, down, down_bias, gain, packed_rows):
+    count, slots, _ = buffer.shape
+    blocks = (count, slots, D)
     return pl.pallas_call(
         expert_kernel,
-        grid=(sources,),
-        in_specs=[
-            block,
-            block,
-            whole(router.shape),
-            whole((D, FF)),
-            whole((1, FF)),
-            whole((FF, D)),
-            whole((1, D)),
-            whole((3, D)),
-        ],
-        out_specs=(
-            block,
-            block,
-            whole((D, FF)),
-            whole((1, FF)),
-            whole((D, FF)),
-            whole((1, D)),
-        ),
-        out_shape=(
-            full((sources, slots, D), BF16),
-            full((sources, slots, D), BF16),
-            full((D, FF)),
-            full((1, FF)),
-            full((D, FF)),
-            full((1, D)),
-        ),
+        out_shape=(full(blocks, BF16), full(blocks, BF16), full((packed_rows, D), BF16)),
         scratch_shapes=[
+            pltpu.VMEM(blocks, BF16),
+            pltpu.VMEM(blocks, BF16),
+            pltpu.VMEM(blocks, BF16),
             pltpu.VMEM((slots, FF), BF16),
             pltpu.VMEM((slots, FF), F32),
-            pltpu.VMEM((8, 128), F32),
+            pltpu.VMEM((D, FF), F32),
+            pltpu.VMEM((D, FF), F32),
+            pltpu.VMEM((1, FF), F32),
+            pltpu.VMEM((1, D), F32),
+            pltpu.SemaphoreType.DMA((3, count)),
+            pltpu.SemaphoreType.DMA((3, count)),
         ],
-        compiler_params=params(),
+        compiler_params=params(collective_id=1, has_side_effects=True),
         name="experts",
-    )(arrived, cot, router, up, up_bias, down, down_bias, gain)
+    )(buffer, cot, router, up, up_bias, down, down_bias, gain)
 
 
 def backward_kernel(
     second, cot, slot_col, routes, outputs, grads, router, first_low, active, slope, n_in, rstd_in,
     up, down, gain, offset,
-    result, grad_first, up_grad, up_bias_grad, down_grad_t, down_bias_grad, router_grad,
+    result, grad_first, packed, up_bias_grad, down_bias_grad, router_grad,
     gain_grad, offset_grad,
-    flat,
+    flat, up_grad, down_grad_t,
 ):
     step = pl.program_id(0)
 
@@ -548,7 +780,7 @@
     grad_gate = jnp.sum(grad_moe * picked, axis=1, keepdims=True)
     grad_logits = grad_gate * gate * (onehot - chances)
     grad_logits_low = grad_logits.astype(BF16)
-    router_grad[...] += dot(x.astype(BF16), grad_logits_low, 0, 0)
+    router_grad[...] += dot(grad_logits_low, x.astype(BF16), 0, 0)
     grad_second = z + dispatched + dot(grad_logits_low, router[...].astype(BF16), 1, 1)
 
     n = n_in[...].astype(F32)
@@ -573,10 +805,16 @@
     for line in range(lines):
         result[line] = flat[line * SIDE : (line + 1) * SIDE, :].astype(BF16)
 
+    @pl.when(step == TOKENS // ROWS - 1)
+    def _():
+        pack_pair(packed, up_grad, down_grad_t)
+        if packed.shape[0] > 2 * FF:
+            packed[2 * FF :, :] = jnp.zeros_like(packed[2 * FF :, :])
+
 
 def backward(
     second, cot, slot_col, routes, outputs, grads, router, first_low, active, slope, n, rstd,
-    up, down, gain, offset,
+    up, down, gain, offset, packed_rows,
 ):
     rows = lambda width: pl.BlockSpec((ROWS, width), lambda i: (i, 0))
     lines = pl.BlockSpec((ROWS // SIDE, SIDE, D), lambda i: (i, 0, 0))
@@ -605,26 +843,28 @@
         out_specs=(
             lines,
             rows(D),
-            whole((D, FF)),
+            whole((packed_rows, D)),
             whole((1, FF)),
-            whole((D, FF)),
             whole((1, D)),
-            whole(router.shape),
+            whole((router.shape[1], D)),
             whole((3, D)),
             whole((3, D)),
         ),
         out_shape=(
             full((SIDE, SIDE, D), BF16),
             full((TOKENS, D)),
-            full((D, FF)),
+            full((packed_rows, D), BF16),
             full((1, FF)),
-            full((D, FF)),
             full((1, D)),
-            full(router.shape),
+            full((router.shape[1], D)),
             full((3, D)),
             full((3, D)),
         ),
-        scratch_shapes=[pltpu.VMEM((ROWS, D), F32)],
+        scratch_shapes=[
+            pltpu.VMEM((ROWS, D), F32),
+            pltpu.VMEM((D, FF), F32),
+            pltpu.VMEM((D, FF), F32),
+        ],
         compiler_params=params(),
         name="backward",
     )(
@@ -636,8 +876,8 @@
 def attend_back_kernel(
     shifts, scale, grad_first, n_in, rstd_in, joint, probs, mixture, win_t, inverse,
     in_weight, out_weight, gain,
-    tokens_grad, in_grad, out_grad, out_bias_grad, gain_grad, offset_grad, scale_grad, table_grad,
-    doubled, windows, joint_grad,
+    tokens_grad, packed, in_bias_grad, out_bias_grad, gain_grad, offset_grad, scale_grad, table_grad,
+    doubled, windows, joint_grad, in_grad, out_grad,
 ):
     window = pl.program_id(0)
     shift_row, shift_col = shifts[0, 0], shifts[0, 1]
@@ -697,11 +937,19 @@
             tokens_grad[row] = line + grad_first[row * SIDE : (row + 1) * SIDE, :]
 
         roll_to_image(windows, doubled, write_row, shift_row, shift_col)
+        for block in range(3):
+            packed[block * D : (block + 1) * D, :] = in_grad[
+                :D, block * D : (block + 1) * D
+            ].astype(BF16)
+        packed[3 * D : 4 * D, :] = out_grad[...].astype(BF16)
+        if packed.shape[0] > 4 * D:
+            packed[4 * D :, :] = jnp.zeros_like(packed[4 * D :, :])
+        in_bias_grad[...] = in_grad[D : D + 1, :]
 
 
 def attend_back(
     shifts, scale, grad_first, n, rstd, joint, probs, mixture, win_t, inverse,
-    in_weight, out_weight, gain,
+    in_weight, out_weight, gain, packed_rows,
 ):
     per_window = lambda *dims: pl.BlockSpec((1,) + dims, lambda w: (w,) + (0,) * len(dims))
     rows = lambda width: pl.BlockSpec((AREA, width), lambda w: (w, 0))
@@ -725,8 +973,8 @@
         ],
         out_specs=(
             whole((SIDE, SIDE, D)),
-            whole((D + 16, 3 * D)),
-            whole((D, D)),
+            whole((packed_rows, D)),
+            whole((1, 3 * D)),
             whole((1, D)),
             whole((1, D)),
             whole((1, D)),
@@ -735,8 +983,8 @@
         ),
         out_shape=(
             full((SIDE, SIDE, D)),
-            full((D + 16, 3 * D)),
-            full((D, D)),
+            full((packed_rows, D), BF16),
+            full((1, 3 * D)),
             full((1, D)),
             full((1, D)),
             full((1, D)),
@@ -747,6 +995,8 @@
             pltpu.VMEM((SIDE, SIDE + WS, D), F32),
             pltpu.VMEM((TOKENS, D), F32),
             pltpu.VMEM((3 * D, AREA), BF16),
+            pltpu.VMEM((D + 16, 3 * D), F32),
+            pltpu.VMEM((D, D), F32),
         ],
         compiler_params=params(),
         name="attend_back",
@@ -756,7 +1006,49 @@
     )
 
 
-def table_back_kernel(table_grad, scale_rows, w1, b1, w2, out1, out2, out3, values_grad):
+SMALL = (
+    ("in_bias", 1, 3 * D),
+    ("out_bias", 1, D),
+    ("up_bias", 1, FF),
+    ("down_bias", 1, D),
+    ("gain_first", 1, D),
+    ("gain_rest", 2, D),
+    ("offset_first", 1, D),
+    ("offset_rest", 2, D),
+    ("table_one", 3, UNITS),
+    ("table_two", HEADS, UNITS),
+    ("scale", HEADS, 128),
+    ("router", 0, D),
+)
+
+
+def small_places(experts):
+    places, at = {}, 0
+    for name, rows, width in SMALL:
+        rows = rows or experts
+        places[name] = (at, rows, width)
+        at += rows * (width // 128)
+    return places, at
+
+
+def put_small(ref, places, name, value):
+    at, rows, width = places[name]
+    for lane in range(0, width, 128):
+        ref[at : at + rows, :] = value[:, lane : lane + 128]
+        at += rows
+
+
+def get_small(ref, places, name):
+    at, rows, width = places[name]
+    return jnp.concatenate(
+        [ref[at + i * rows : at + (i + 1) * rows, :] for i in range(width // 128)], axis=1
+    )
+
+
+def table_back_kernel(
+    places, table_grad, scale_rows, w1, b1, w2, in_bias, out_bias, up_bias, down_bias,
+    gain_first, gain_rest, offset_first, offset_rest, router, small, values_grad,
+):
     spread = spread_matrix(True)
     for head in range(HEADS):
         high, low = split(table_grad[head])
@@ -777,23 +1069,136 @@
     hidden, slope = gelu_pair(w1t[:, 0:1] * f_row + w1t[:, 1:2] * f_col + b1t[:, 0:1])
     chance = jax.nn.sigmoid(exact_dot(w2[...], hidden, 0, 0))
     grad_pre = values_grad[:HEADS, :] * (16.0 * chance * (1.0 - chance))
-    out2[...] = exact_dot(hidden, grad_pre, 1, 1)
+    small[...] = jnp.zeros_like(small)
+    put_small(small, places, "table_two", exact_dot(grad_pre, hidden, 1, 1))
     grad_hidden = exact_dot(w2[...], grad_pre, 1, 0) * slope
     f_row, f_col = offsets_row((8, TABLE), 1, -1.0)
     kind = iota((8, TABLE), 0)
     factors = jnp.where(kind == 0, f_row, jnp.where(kind == 1, f_col, 1.0))
-    out1[...] = exact_dot(factors, grad_hidden, 1, 1)
-    out3[...] = jnp.sum(scale_rows[...], axis=1, keepdims=True)
-
-
-def table_back(table_grad, scale_rows, w1, b1, w2):
+    put_small(small, places, "table_one", exact_dot(factors, grad_hidden, 1, 1)[:3, :])
+    scales = jnp.sum(scale_rows[...], axis=1, keepdims=True)
+    put_small(small, places, "scale", jnp.broadcast_to(scales, (HEADS, 128)))
+    put_small(small, places, "in_bias", in_bias[...])
+    put_small(small, places, "out_bias", out_bias[...])
+    put_small(small, places, "up_bias", up_bias[...])
+    put_small(small, places, "down_bias", down_bias[...])
+    put_small(small, places, "gain_first", gain_first[...])
+    put_small(small, places, "gain_rest", gain_rest[1:, :])
+    put_small(small, places, "offset_first", offset_first[...])
+    put_small(small, places, "offset_rest", offset_rest[1:, :])
+    put_small(small, places, "router", router[...])
+
+
+def table_back(small_rows, experts, *args):
+    places, _ = small_places(experts)
     return pl.pallas_call(
-        table_back_kernel,
-        out_shape=(full((8, UNITS)), full((UNITS, HEADS)), full((HEADS, 1))),
+        functools.partial(table_back_kernel, places),
+        out_shape=full((small_rows, 128)),
         scratch_shapes=[pltpu.VMEM((16, TABLE), F32)],
         compiler_params=params(),
         name="table_back",
-    )(table_grad, scale_rows, w1, b1, w2)
+    )(*args)
+
+
+def reduce_kernel(names, *refs):
+    count = len(names)
+    sources, outs, refs = refs[:count], refs[count : 2 * count], refs[2 * count :]
+    sums = []
+    for name, source, out in zip(names, sources, outs):
+        levels = levels_of(name)
+        depth = len(levels)
+        held, lands, (send, recv) = refs[0], refs[1 : 1 + depth], refs[1 + depth : 3 + depth]
+        refs = refs[3 + depth :]
+        sums.append(Sum(source, held, out, lands, send, recv, levels).stages())
+    greet(greeted(levels_of(("dp", "expert"))))
+    for k in range(max(len(stages) for stages in sums)):
+        for stages in sums:
+            if k < len(stages):
+                stages[k]()
+
+
+def reduce_all(names, arrays, dp, experts):
+    scratch = []
+    for name, array in zip(names, arrays):
+        counts = level_counts(name, dp, experts)
+        scratch.append(pltpu.VMEM(array.shape, array.dtype))
+        scratch += land_shapes(array.shape[0], array.shape[1], array.dtype, counts)
+        scratch += sum_sems(counts)
+    return pl.pallas_call(
+        functools.partial(reduce_kernel, names),
+        out_shape=tuple(full(array.shape, array.dtype) for array in arrays),
+        scratch_shapes=scratch,
+        compiler_params=params(collective_id=2, has_side_effects=True),
+        name="reduce",
+    )(*arrays)
+
+
+def unpack_kernel(
+    places, own, dense, last, small,
+    in_grad, in_bias, scale, table_first, table_first_bias, table_second, out_grad, out_bias,
+    up_grad, up_bias, down_grad, down_bias, router, own_up, own_up_bias, own_down, own_down_bias,
+    gain, offset,
+):
+    for block in range(3):
+        part = slice(block * D, (block + 1) * D)
+        in_grad[:, part] = last[part, :].astype(F32)
+    out_grad[...] = last[3 * D : 4 * D, :].astype(F32)
+    for source, up, down in ((dense, up_grad, down_grad), (own, own_up, own_down)):
+        for block in range(FF // D):
+            part = slice(block * D, (block + 1) * D)
+            up[:, part] = source[part, :].astype(F32)
+            down[part, :] = source[FF + block * D : FF + (block + 1) * D, :].astype(F32)
+    tail = own[2 * FF : 2 * FF + 16, :].astype(F32)
+    for block in range(FF // D):
+        own_up_bias[:, block * D : (block + 1) * D] = tail[block : block + 1, :]
+    own_down_bias[...] = tail[FF // D : FF // D + 1, :]
+    get = functools.partial(get_small, small, places)
+    row = get("in_bias")
+    in_bias[0:1, :] = row[:, :D]
+    in_bias[1:2, :] = row[:, 2 * D :]
+    scale[...] = get("scale")[:, 0:1]
+    one = get("table_one")
+    table_first[...] = one[0:2, :]
+    table_first_bias[...] = one[2:3, :]
+    table_second[...] = jnp.transpose(get("table_two"), (1, 0))
+    out_bias[...] = get("out_bias")
+    up_bias[...] = get("up_bias")
+    down_bias[...] = get("down_bias")
+    router[...] = jnp.transpose(get("router"), (1, 0))
+    gain[0:1, :] = get("gain_first")
+    gain[1:3, :] = get("gain_rest")
+    offset[0:1, :] = get("offset_first")
+    offset[1:3, :] = get("offset_rest")
+
+
+def unpack(own, dense, last, small, experts):
+    places, _ = small_places(experts)
+    return pl.pallas_call(
+        functools.partial(unpack_kernel, places),
+        out_shape=(
+            full((D, 3 * D)),
+            full((2, D)),
+            full((HEADS, 1)),
+            full((2, UNITS)),
+            full((1, UNITS)),
+            full((UNITS, HEADS)),
+            full((D, D)),
+            full((1, D)),
+            full((D, FF)),
+            full((1, FF)),
+            full((FF, D)),
+            full((1, D)),
+            full((D, experts)),
+            full((D, FF)),
+            full((1, FF)),
+            full((FF, D)),
+            full((1, D)),
+            full((3, D)),
+            full((3, D)),
+        ),
+        compiler_params=params(),
+        name="unpack",
+    )(own, dense, last, small)
 
 
 def per_device(
@@ -803,8 +1208,17 @@
     expert_up, expert_up_bias, expert_down, expert_down_bias, norm_gain, norm_bias,
 ):
     experts = router_weight.shape[1]
+    dp = lax.axis_size("dp")
+    group = lax.axis_size("expert")
     capacity = (5 * TOKENS + 4 * experts - 1) // (4 * experts)
     slots = -(-capacity // 16) * 16
+    own, both = ("dp",), ("dp", "expert")
+    own_counts, both_counts = level_counts(own, dp, group), level_counts(both, dp, group)
+    own_rows = padded_rows(2 * FF + 16, own_counts, 16)
+    dense_rows = padded_rows(2 * FF, both_counts, 16)
+    last_rows = padded_rows(4 * D, both_counts, 16)
+    small_rows = padded_rows(small_places(experts)[1], both_counts, 8)
+
     picture = tokens.reshape(SIDE, SIDE, D)
     cot = cotangent.reshape(SIDE, SIDE, D)
     route_col = routes.reshape(TOKENS, 1)
@@ -814,94 +1228,68 @@
         route_col, cot, bias_net_first_weight, first_bias, bias_net_second_weight,
         logit_scale.reshape(1, HEADS), experts, capacity, slots,
     )
-    exchange = lambda blocks: lax.all_to_all(
-        blocks, "expert", split_axis=0, concat_axis=0, tiled=True
-    )
-    cot_arrived = exchange(cot_slots)
-    normed, n_zero, rstd_zero, joint, probs, mixture, win_t, inverse = attend(
-        shifts, scale, picture, in_weight, in_bias, table,
+    cot_arrived, normed, n_zero, rstd_zero, joint, probs, mixture, win_t, inverse = attend(
+        cot_slots, shifts, scale, picture, in_weight, in_bias, table,
         out_weight, out_bias.reshape(1, D), norm_gain, norm_bias,
     )
     first_low, active, slope, n_one, rstd_one, second, buffer = forward(
         shifts, picture, normed, up_weight, up_bias.reshape(1, FF), down_weight,
         down_bias.reshape(1, D), norm_gain, norm_bias, slot_row, experts, slots,
     )
-    arrived = exchange(buffer)
+    returned, grad_returned, own_packed = run_experts(
+        buffer, cot_arrived, router_weight, expert_up[0], expert_up_bias, expert_down[0],
+        expert_down_bias, norm_gain, own_rows,
+    )
     (
-        produced, grad_arrived, expert_up_grad, expert_up_bias_grad, expert_down_grad_t,
-        expert_down_bias_grad,
-    ) = run_experts(
-        arrived, cot_arrived, router_weight, expert_up[0], expert_up_bias, expert_down[0],
-        expert_down_bias, norm_gain,
-    )
-    returned = exchange(produced).reshape(-1, D)
-    grad_returned = exchange(grad_arrived).reshape(-1, D)
-    (
-        result, grad_first, up_grad, up_bias_grad, down_grad_t, down_bias_grad, router_grad,
+        result, grad_first, dense_packed, up_bias_grad, down_bias_grad, router_grad,
         gain_grad, offset_grad,
     ) = backward(
-        second, cot, slot_col, route_col, returned, grad_returned, router_weight, first_low,
-        active, slope, n_one, rstd_one, up_weight, down_weight, norm_gain, norm_bias,
+        second, cot, slot_col, route_col, returned.reshape(-1, D), grad_returned.reshape(-1, D),
+        router_weight, first_low, active, slope, n_one, rstd_one, up_weight, down_weight,
+        norm_gain, norm_bias, dense_rows,
     )
     (
-        tokens_grad, in_grad, out_grad, out_bias_grad, gain_zero, offset_zero, scale_rows,
+        tokens_grad, last_packed, in_bias_grad, out_bias_grad, gain_zero, offset_zero, scale_rows,
         table_grad,
     ) = attend_back(
         shifts, scale, grad_first, n_zero, rstd_zero, joint, probs, mixture, win_t, inverse,
-        in_weight, out_weight, norm_gain,
-    )
-    table_one, table_two, scale_grad = table_back(
-        table_grad, scale_rows, bias_net_first_weight, first_bias, bias_net_second_weight
-    )
-
-    low_sum = lambda parts, axes: [
-        part.astype(F32)
-        for part in lax.psum([part.astype(BF16) for part in parts], axes)
-    ]
-    expert_up_grad, expert_down_grad_t, expert_up_bias_grad, expert_down_bias_grad = low_sum(
-        [expert_up_grad, expert_down_grad_t, expert_up_bias_grad, expert_down_bias_grad], "dp"
-    )
-    both = ("dp", "expert")
-    up_grad, down_grad_t = low_sum([up_grad, down_grad_t], both)
-    in_weight_grad, out_grad = low_sum([in_grad[:D], out_grad], both)
-    smalls = [
-        in_grad[D], out_bias_grad, up_bias_grad, down_bias_grad, router_grad,
-        gain_zero, gain_grad[1:], offset_zero, offset_grad[1:],
-        table_one[:3], table_two, scale_grad,
-    ]
-    sizes = [small.size for small in smalls]
-    packed = lax.psum(jnp.concatenate([small.reshape(-1) for small in smalls]), both)
-    pieces = []
-    at = 0
-    for size in sizes:
-        pieces.append(packed[at : at + size])
-        at += size
+        in_weight, out_weight, norm_gain, last_rows,
+    )
+    small = table_back(
+        small_rows, experts, table_grad, scale_rows, bias_net_first_weight, first_bias,
+        bias_net_second_weight, in_bias_grad, out_bias_grad, up_bias_grad, down_bias_grad,
+        gain_zero, gain_grad, offset_zero, offset_grad, router_grad,
+    )
+    sums = reduce_all(
+        (own, both, both, both), (own_packed, dense_packed, last_packed, small), dp, group
+    )
     (
-        in_bias_all, out_bias_grad, up_bias_grad, down_bias_grad, router_grad,
-        gain_zero, gain_rest, offset_zero, offset_rest, table_one, table_two, scale_grad,
-    ) = pieces
+        in_weight_grad, in_bias_grad, scale_grad, table_one, table_bias, table_two, out_grad,
+        out_bias_grad, up_grad, up_bias_grad, down_grad, down_bias_grad, router_grad,
+        own_up, own_up_bias, own_down, own_down_bias, gain_grad, offset_grad,
+    ) = unpack(*sums, experts)
     return (
         result.reshape(tokens.shape),
         tokens_grad.reshape(tokens.shape),
         in_weight_grad,
-        jnp.stack([in_bias_all[:D], in_bias_all[2 * D :]]),
-        scale_grad,
-        table_one[: 2 * UNITS].reshape(2, UNITS),
-        table_one[2 * UNITS :],
-        table_two.reshape(UNITS, HEADS),
+        in_bias_grad,
+        scale_grad.reshape(HEADS),
+        table_one,
+        table_bias.reshape(UNITS),
+        table_two,
         out_grad,
-        out_bias_grad,
+        out_bias_grad.reshape(D),
         up_grad,
-        up_bias_grad,
-        down_grad_t.T,
-        down_bias_grad,
-        router_grad.reshape(D, experts),
-        expert_up_grad[None],
-        expert_up_bias_grad,
-        expert_down_grad_t.T[None],
-        expert_down_bias_grad,
-        jnp.concatenate([gain_zero, gain_rest]).reshape(3, D),
-        jnp.concatenate([offset_zero, offset_rest]).reshape(3, D),
+        up_bias_grad.reshape(FF),
+        down_grad,
+        down_bias_grad.reshape(D),
+        router_grad,
+        own_up[None],
+        own_up_bias,
+        own_down[None],
+        own_down_bias,
+        gain_grad,
+        offset_grad,
     )
 
 

time: 490 us -> 388 us (0.79)
  the two profiles are of different devices: /device:TPU:0 before, /device:TPU:25 now
where the time goes in v2:
time: 388 us; the launch traced here: 383 us
  Pallas kernels  362 us (93%)
  local copies, waits for them, and re-layouts  15.4 us (4%)
  other arithmetic  5.18 us (1%)
    pallas_call x1, Pallas kernels, reduce_all(): pl.pallas_call(functools.partial(reduce_kernel, names), out_shape=tuple((...  113 us
    pallas_call x1, Pallas kernels, attend_back(): pl.pallas_call(attend_back_kernel, grid=(WINDOWS,), in_specs=[smem(), sme...  63 us
    pallas_call x1, Pallas kernels, attend(): pl.pallas_call(attend_kernel, grid=(WINDOWS,), in_specs=[pl.BlockSpec(mem...  62.1 us
    pallas_call x1, Pallas kernels, run_experts(): pl.pallas_call(expert_kernel, out_shape=(full(blocks, BF16), full(blocks,...  50.2 us
    pallas_call x1, Pallas kernels, backward(): pl.pallas_call(backward_kernel, grid=(TOKENS // ROWS,), in_specs=[rows(D)...  28.3 us
    pallas_call x1, Pallas kernels, forward(): pl.pallas_call(forward_kernel, grid=(TOKENS // ROWS,), in_specs=[smem(),...  19.1 us
    unnamed x7, local copies, waits for them, and re-layouts  9.74 us
    pallas_call x1, Pallas kernels, prep(): pl.pallas_call(functools.partial(prep_kernel, capacity), out_shape=(full(...  9.49 us

profile of v2, /device:TPU:25, one launch (start us, length us, event | category | flops | bytes accessed | tf_op | source)
XLA Modules:
  0.0 383.2 jit_solution(17158212679211477940)
XLA Ops:
  0.7 1.2 reshape.98.out_bias
  1.9 1.2 reshape.100.down_bias
  3.1 1.3 reshape.99.up_bias
  4.4 1.5 copy.53.router
  5.9 1.6 copy.52.w2
  7.5 1.8 copy.51.routes
  9.4 9.5 %prep.1 = (s32[1296,1]{1,0:T(8,128)}, s32[1,1296]{1,0:T(1,128)}, bf16[4,416,384]{2,1,0:T(8,128)(2,1)}, f32[12,144,144]{2,1,0:T(8,128)}, f32[1,12]{1,0:T(1,128)}) custom-call(s32[1296,1]{1,0:T(8,128)} %copy.51.routes, bf16[36,36,384]{2,1,0:T(8,128)(2,1)} %bitcast.14, f32[2,512]{1,0:T(2,128)} %w1.3, f32[1,512]{1,0:T(1,128)} %bitcast.23, f32[512,12]{1,0:T(8,128)} %copy.52.w2, ...), custom_call_target="tpu_custom_call" | custom-call | tf_op jit(solution)/shard_map/prep/pallas_call | solution.py:323
  18.9 62.1 %attend.1 = (bf16[4,416,384]{2,1,0:T(8,128)(2,1)}, f32[1296,384]{1,0:T(8,128)}, bf16[1296,384]{1,0:T(8,128)(2,1)}, f32[1296,1]{1,0:T(8,128)}, bf16[9,1152,144]{2...) custom-call(bf16[4,416,384]{2,1,0:T(8,128)(2,1)} %get-tuple-element., ...), custom_call_target="tpu_custom_call" | custom-call | tf_op jit(solution)/shard_map/attend/pallas_call | solution.py:462
  81.0 19.1 %forward.1 = (bf16[1296,384]{1,0:T(8,128)(2,1)}, bf16[1296,1536]{1,0:T(8,128)(2,1)}, bf16[1296,1536]{1,0:T(8,128)(2,1)}, bf16[1296,384]{1,0:T(8,128)(2,1)}, f32[...) custom-call(s32[1,2]{1,0:T(1,128)} %shifts.5, bf16[36,36,384]{2,1,0:T(8,128)(2,1)} %bitcast.17, ...), custom_call_target="tpu_custom_call" | custom-call | tf_op jit(solution)/shard_map/forward/pallas_call | solution.py:559
  100.1 50.2 %experts.1 = (bf16[4,416,384]{2,1,0:T(8,128)(2,1)}, bf16[4,416,384]{2,1,0:T(8,128)(2,1)}, bf16[3200,384]{1,0:T(8,128)(2,1)}) custom-call(bf16[4,416,384]{2,1,0:T(8,128)(2,1)} %get-tuple-element.91.buffer, bf16[4,416,384]{2,1,0:T(8,128)(2,1)} %get-tuple-element.92.cot, f32[384,4]{1,0:T(8,128)} %copy.53.router, bf16[384,1536]{1,0:T(8,128)(2,1)} %bitcast.21, ...), custom_call_target="tpu_custom_call" | custom-call | tf_op jit(solution)/shard_map/experts/pallas_call | solution.py:723
  150.3 28.3 %backward.1 = (bf16[36,36,384]{2,1,0:T(8,128)(2,1)}, f32[1296,384]{1,0:T(8,128)}, bf16[3072,384]{1,0:T(8,128)(2,1)}, f32[1,1536]{1,0:T(1,128)}, f32[1,384]{1,0:T...) custom-call(f32[1296,384]{1,0:T(8,128)} %get-tuple-element.89.second, ...), custom_call_target="tpu_custom_call" | custom-call | tf_op jit(solution)/shard_map/backward/pallas_call | solution.py:822
  178.7 63.0 %attend_back.1 = (f32[36,36,384]{2,1,0:T(8,128)}, bf16[1536,384]{1,0:T(8,128)(2,1)}, f32[1,1152]{1,0:T(1,128)}, f32[1,384]{1,0:T(1,128)}, f32[1,384]{1,0:T(1,128...) custom-call(s32[1,2]{1,0:T(1,128)} %shifts.5, f32[1,12]{1,0:T(1,128)} %get-tuple-element.85.scale, ...), custom_call_target="tpu_custom_call" | custom-call | tf_op jit(solution)/shard_map/attend_back/pallas_call | solution.py:956
  241.7 0.0 copy-start
  241.7 8.7 %table_back.1.refs_3_ = f32[256,128]{1,0:T(8,128)} custom-call(f32[12,144,144]{2,1,0:T(8,128)} %get-tuple-element.113.table_grad, f32[12,144]{1,0:T(8,128)} %get-tuple-element.114.scale_rows, f32[2,512]{1,0:T(2,128)} %w1.3, f32[1,512]{1,0:T(1,128)} %bitcast.24, f32[512,12]{1,0:T(8,128)} %copy.52.w2, f32[1,1152]{1,0:T(1,128)} %get-tuple-element.115.in_bias, ...), custom_call_target="tpu_custom_call" | custom-call | tf_op jit(solution)/shard_map/table_back/pallas_call | solution.py:1094
  250.4 0.0 copy-done
  250.4 3.3 copy.57
  253.7 113.3 %reduce.5 = (bf16[3200,384]{1,0:T(8,128)(2,1)}, bf16[3072,384]{1,0:T(8,128)(2,1)}, bf16[1536,384]{1,0:T(8,128)(2,1)}, f32[256,128]{1,0:T(8,128)}) custom-call(bf16[3200,384]{1,0:T(8,128)(2,1)} %get-tuple-element.110.refs_0_, bf16[3072,384]{1,0:T(8,128)(2,1)} %get-tuple-element.111.refs_1_, bf16[1536,384]{1,0:T(8,128)(2,1)} %get-tuple-element.112.refs_2_, ...), custom_call_target="tpu_custom_call" | custom-call | tf_op jit(solution)/shard_map/reduce/pallas_call | solution.py:1127
  367.0 7.5 %unpack.1 = (f32[384,1152]{1,0:T(8,128)}, f32[2,384]{1,0:T(2,128)}, f32[12,1]{1,0:T(8,128)}, f32[2,512]{1,0:T(2,128)}, f32[1,512]{1,0:T(1,128)}, /*index=5*/f32[...) custom-call(bf16[3200,384]{1,0:T(8,128)(2,1)} %get-tuple-element.124, ...), custom_call_target="tpu_custom_call" | custom-call | tf_op jit(solution)/shard_map/unpack/pallas_call | solution.py:1176
  374.5 1.3 reduce.1
  375.8 1.3 reduce.2
  377.1 1.3 reduce.4
  378.3 1.3 reduce.3
  379.6 1.6 copy.59
  381.3 1.7 copy.58
Async XLA Ops:
  241.7 8.7 %copy-start = (f32[36,36,384]{2,1,0:T(8,128)S(1)}, f32[36,36,384]{2,1,0:T(8,128)}, u32[]{:S(2)}) copy-start(f32[36,36,384]{2,1,0:T(8,128)} %get-tuple-element.109) | copy-start | bytes 5971972

commit v3 on v2

--- a/solution.py
+++ b/solution.py
@@ -78,6 +78,10 @@
         - jnp.mean(grad_n, axis=-1, keepdims=True)
         - n * jnp.mean(grad_n * n, axis=-1, keepdims=True)
     )
+
+
+def row_of(ref):
+    return ref[...].reshape(1, ref.shape[0])
 
 
 def col_sum(values):
@@ -275,20 +279,23 @@
 
 
 def prep_kernel(
-    capacity, routes, cot, w1, b1, w2, ls, slot_col, slot_row, zbuf, table, scale, flat, u_ref
+    capacity, routes, cot, w1, b1, w2, ls, slot_col, slot_row, zbuf, table, scale, flat, u_ref, route_col
 ):
     slots = zbuf.shape[1]
     experts = zbuf.shape[0]
+    route_col[...] = jnp.transpose(
+        jnp.broadcast_to(routes[...].astype(F32), (128, TOKENS)), (1, 0)
+    )
     before = (iota((AREA, AREA), 1) < iota((AREA, AREA), 0)).astype(BF16)
     carry = jnp.zeros((1, 128), F32)
     for block in range(TOKENS // AREA):
         rows = pl.ds(block * AREA, AREA)
-        route = routes[rows, :]
-        onehot = (route == iota((AREA, 128), 1)).astype(F32)
+        route = route_col[rows, 0:1]
+        onehot = (route == iota((AREA, 128), 1).astype(F32)).astype(F32)
         ahead = dot(before, onehot.astype(BF16), 1, 0) + carry
         position = jnp.sum(ahead * onehot, axis=1, keepdims=True)
         carry = carry + col_sum(onehot)
-        slot = route.astype(F32) * slots + position
+        slot = route * slots + position
         slot_col[rows, :] = jnp.where(position < capacity, slot, -1.0).astype(I32)
     slot_row[...] = jnp.transpose(
         jnp.broadcast_to(slot_col[...].astype(F32), (TOKENS, 128)), (1, 0)
@@ -301,12 +308,12 @@
         pick = (iota((slots, TOKENS), 0) + expert * slots == slot_row[...]).astype(BF16)
         zbuf[expert] = dot(pick, low, 1, 0).astype(BF16)
 
-    scale[...] = jnp.exp(ls[...])
+    scale[...] = jnp.exp(row_of(ls))
     f_row, f_col = offsets_row((UNITS, TABLE), 1, 1.0)
     w1t = jnp.transpose(w1[...], (1, 0))
-    b1t = jnp.transpose(b1[...], (1, 0))
+    b1t = jnp.transpose(row_of(b1), (1, 0))
     hidden, _ = gelu_pair(w1t[:, 0:1] * f_row + w1t[:, 1:2] * f_col + b1t[:, 0:1])
-    values = 16.0 * jax.nn.sigmoid(exact_dot(w2[...], hidden, 0, 0))
+    values = 16.0 * jax.nn.sigmoid(exact_dot(w2[...], hidden, 1, 0))
     spread = spread_matrix(False).astype(BF16)
     for head in range(HEADS):
         line = jnp.broadcast_to(values[head : head + 1, :], (16, TABLE))
@@ -329,7 +336,11 @@
             full((HEADS, AREA, AREA)),
             full((1, HEADS)),
         ),
-        scratch_shapes=[pltpu.VMEM((TOKENS, D), F32), pltpu.VMEM((AREA, 384), F32)],
+        scratch_shapes=[
+            pltpu.VMEM((TOKENS, D), F32),
+            pltpu.VMEM((AREA, 384), F32),
+            pltpu.VMEM((TOKENS, 128), F32),
+        ],
         compiler_params=params(),
         name="prep",
     )(routes, cotangent, w1, b1, w2, ls)
@@ -382,7 +393,7 @@
 def attend_kernel(
     cot_slots, shifts, scale, tokens, in_weight, in_bias, table, out_weight, out_bias, gain, offset,
     cot_arrived, normed, n_out, rstd_out, joint, probs, mixture, win_t, inverse,
-    doubled, windows, in_weight_t, bias_col, send, recv, local,
+    doubled, windows, in_weight_t, bias_col, joined, send, recv, local,
 ):
     window = pl.program_id(0)
     shift_row, shift_col = shifts[0, 0], shifts[0, 1]
@@ -419,29 +430,51 @@
     win_t[0, D:, :] = (iota((16, AREA), 0) == 0).astype(BF16)
     label_keys, label_queries = window_labels(window, shift_row, shift_col)
     mask = jnp.where(label_keys == label_queries, 0.0, -100.0)
-    for head in range(HEADS):
-        at = head * HEAD
-        query = dot(in_weight_t[at : at + HEAD, :], mine, 1, 1) + bias_col[at : at + HEAD, 0:1]
-        key = dot(in_weight_t[D + at : D + at + HEAD, :], mine, 1, 1)
-        value = (
-            dot(in_weight_t[2 * D + at : 2 * D + at + HEAD, :], mine, 1, 1)
-            + bias_col[at : at + HEAD, 1:2]
-        ).astype(BF16)
-        query_inverse = lax.rsqrt(1.0 + col_sum(query * query))
-        key_inverse = lax.rsqrt(1.0 + col_sum(key * key))
-        query = (query * query_inverse).astype(BF16)
-        key = (key * key_inverse).astype(BF16)
-        scores = dot(key, query, 0, 0) * scale[0, head] + (table[head] + mask)
-        exponent = jnp.exp(scores - jnp.max(scores, axis=0, keepdims=True))
-        low = (exponent * (1.0 / col_sum(exponent))).astype(BF16)
-        mixture[0, at : at + HEAD, :] = dot(value, low, 1, 0).astype(BF16)
-        probs[0, head] = low
-        joint[0, at : at + HEAD, :] = query
-        joint[0, D + at : D + at + HEAD, :] = key
-        joint[0, 2 * D + at : 2 * D + at + HEAD, :] = value
-        inverse[0, head : head + 1, :] = query_inverse
-        inverse[0, HEADS + head : HEADS + head + 1, :] = key_inverse
-    branch = dot(mixture[0], out_weight[...], 0, 0) + out_bias[...]
+    joined[...] = dot(in_weight_t[...], mine, 1, 1)
+
+    def unit(rows, bias, place):
+        shaped = (joined[rows, :] + bias).reshape(HEADS, HEAD, AREA)
+        inner = lax.rsqrt(1.0 + jnp.sum(shaped * shaped, axis=1, keepdims=True))
+        for head in range(HEADS):
+            inverse[0, place + head : place + head + 1, :] = inner[head]
+        return (shaped * inner).reshape(D, AREA).astype(BF16)
+
+    queries = unit(slice(0, D), bias_col[:, 0:1], 0)
+    keys = unit(slice(D, 2 * D), 0.0, HEADS)
+    values = (joined[2 * D :, :] + bias_col[:, 1:2]).astype(BF16)
+    joint[0, :D, :] = queries
+    joint[0, D : 2 * D, :] = keys
+    joint[0, 2 * D :, :] = values
+    key_rows = jnp.transpose(keys, (1, 0))
+    blank = jnp.zeros((HEAD, AREA), BF16)
+
+    def scores_of(group):
+        lanes = key_rows[:, group * 128 : (group + 1) * 128]
+        found = []
+        for head in range(4):
+            at = group * 128 + head * HEAD
+            parts = [blank] * 4
+            parts[head] = queries[at : at + HEAD, :]
+            found.append(dot(lanes, jnp.concatenate(parts, axis=0), 1, 0))
+        return found
+
+    ahead = scores_of(0)
+    for group in range(HEADS // 4):
+        current = ahead
+        if group + 1 < HEADS // 4:
+            ahead = scores_of(group + 1)
+        lows = []
+        for i in range(4):
+            head = group * 4 + i
+            scores = current[i] * scale[0, head] + (table[head] + mask)
+            exponent = jnp.exp(scores - jnp.max(scores, axis=0, keepdims=True))
+            low = (exponent * (1.0 / col_sum(exponent))).astype(BF16)
+            probs[0, head] = low
+            lows.append(low)
+        for i in range(4):
+            at = (group * 4 + i) * HEAD
+            mixture[0, at : at + HEAD, :] = dot(values[at : at + HEAD, :], lows[i], 1, 0).astype(BF16)
+    branch = dot(mixture[0], out_weight[...], 0, 0) + row_of(out_bias)
     n, rstd = norm_parts(branch)
     normed[...] = n * gain[0:1, :] + offset[0:1, :]
     n_out[...] = n.astype(BF16)
@@ -471,7 +504,7 @@
             whole((2, D)),
             whole((HEADS, AREA, AREA)),
             whole((D, D)),
-            whole((1, D)),
+            whole((D,)),
             whole((3, D)),
             whole((3, D)),
         ],
@@ -502,6 +535,7 @@
             pltpu.VMEM((TOKENS, D), F32),
             pltpu.VMEM((3 * D, D), BF16),
             pltpu.VMEM((D, 128), F32),
+            pltpu.VMEM((3 * D, AREA), F32),
             pltpu.SemaphoreType.DMA((cot_slots.shape[0],)),
             pltpu.SemaphoreType.DMA((cot_slots.shape[0],)),
             pltpu.SemaphoreType.DMA(()),
@@ -529,9 +563,10 @@
     first = image[rows, :]
     low = first.astype(BF16)
     first_low[...] = low
-    branch = jnp.broadcast_to(down_bias[...], (ROWS, D))
+    up_row = row_of(up_bias)
+    branch = jnp.broadcast_to(row_of(down_bias), (ROWS, D))
     for at in range(0, FF, CHUNK):
-        hidden = dot(low, up[:, at : at + CHUNK], 1, 0) + up_bias[:, at : at + CHUNK]
+        hidden = dot(low, up[:, at : at + CHUNK], 1, 0) + up_row[:, at : at + CHUNK]
         activated, derivative = gelu_pair(hidden)
         activated = activated.astype(BF16)
         active[:, at : at + CHUNK] = activated
@@ -564,9 +599,9 @@
             whole((SIDE, SIDE, D)),
             whole((TOKENS, D)),
             whole((D, FF)),
-            whole((1, FF)),
+            whole((FF,)),
             whole((FF, D)),
-            whole((1, D)),
+            whole((D,)),
             whole((3, D)),
             whole((3, D)),
             whole((1, TOKENS)),
@@ -647,7 +682,7 @@
             move(0, step, buffer.at[owner], arrived.at[step], owner).wait_recv()
 
         features = arrived[step]
-        logits = dot(features, router_high, 1, 0) + dot(features, router_low, 1, 0)
+        logits = dot(features, router_high, 1, 1) + dot(features, router_low, 1, 1)
         chances = jnp.exp(logits - jnp.max(logits, axis=1, keepdims=True))
         own = jnp.where(iota(chances.shape, 1) == me, chances, 0.0)
         gate = jnp.sum(own, axis=1, keepdims=True) / jnp.sum(chances, axis=1, keepdims=True)
@@ -742,7 +777,7 @@
 
 
 def backward_kernel(
-    second, cot, slot_col, routes, outputs, grads, router, first_low, active, slope, n_in, rstd_in,
+    second, cot, slot_col, outputs, grads, router, first_low, active, slope, n_in, rstd_in,
     up, down, gain, offset,
     result, grad_first, packed, up_bias_grad, down_bias_grad, router_grad,
     gain_grad, offset_grad,
@@ -767,10 +802,12 @@
     picked = dot(pick, outputs[...], 1, 0)
     dispatched = dot(pick, grads[...], 1, 0)
 
-    logits = exact_dot(x, router[...], 1, 0)
+    logits = exact_dot(x, router[...], 1, 1)
     chances = jnp.exp(logits - jnp.max(logits, axis=1, keepdims=True))
     chances = chances / jnp.sum(chances, axis=1, keepdims=True)
-    onehot = (routes[...] == iota(chances.shape, 1)).astype(F32)
+    slots = slots_all // chances.shape[1]
+    within = slot_col[...] - iota(chances.shape, 1) * slots
+    onehot = ((within >= 0) & (within < slots)).astype(F32)
     gate = jnp.sum(chances * onehot, axis=1, keepdims=True)
     n, rstd = norm_parts(gate * picked)
     final = x + n * gain[2:3, :] + offset[2:3, :]
@@ -781,7 +818,7 @@
     grad_logits = grad_gate * gate * (onehot - chances)
     grad_logits_low = grad_logits.astype(BF16)
     router_grad[...] += dot(grad_logits_low, x.astype(BF16), 0, 0)
-    grad_second = z + dispatched + dot(grad_logits_low, router[...].astype(BF16), 1, 1)
+    grad_second = z + dispatched + dot(grad_logits_low, router[...].astype(BF16), 1, 0)
 
     n = n_in[...].astype(F32)
     gain_grad[1:2, :] += col_sum(grad_second * n)
@@ -813,7 +850,7 @@
 
 
 def backward(
-    second, cot, slot_col, routes, outputs, grads, router, first_low, active, slope, n, rstd,
+    second, cot, slot_col, outputs, grads, router, first_low, active, slope, n, rstd,
     up, down, gain, offset, packed_rows,
 ):
     rows = lambda width: pl.BlockSpec((ROWS, width), lambda i: (i, 0))
@@ -825,7 +862,6 @@
         in_specs=[
             rows(D),
             lines,
-            rows(1),
             rows(1),
             whole((slots_all, D)),
             whole((slots_all, D)),
@@ -846,7 +882,7 @@
             whole((packed_rows, D)),
             whole((1, FF)),
             whole((1, D)),
-            whole((router.shape[1], D)),
+            whole(router.shape),
             whole((3, D)),
             whole((3, D)),
         ),
@@ -856,7 +892,7 @@
             full((packed_rows, D), BF16),
             full((1, FF)),
             full((1, D)),
-            full((router.shape[1], D)),
+            full(router.shape),
             full((3, D)),
             full((3, D)),
         ),
@@ -868,7 +904,7 @@
         compiler_params=params(),
         name="backward",
     )(
-        second, cot, slot_col, routes, outputs, grads, router, first_low, active, slope, n, rstd,
+        second, cot, slot_col, outputs, grads, router, first_low, active, slope, n, rstd,
         up, down, gain, offset,
     )
 
@@ -877,7 +913,7 @@
     shifts, scale, grad_first, n_in, rstd_in, joint, probs, mixture, win_t, inverse,
     in_weight, out_weight, gain,
     tokens_grad, packed, in_bias_grad, out_bias_grad, gain_grad, offset_grad, scale_grad, table_grad,
-    doubled, windows, joint_grad, in_grad, out_grad,
+    doubled, windows, joint_grad, grads_f32, in_grad, out_grad,
 ):
     window = pl.program_id(0)
     shift_row, shift_col = shifts[0, 0], shifts[0, 1]
@@ -902,32 +938,57 @@
     grad_low = grad_branch.astype(BF16)
     out_bias_grad[...] += col_sum(grad_branch)
     out_grad[...] += dot(mixture[0], grad_low, 1, 0)
+    grad_mixture = dot(out_weight[...], grad_low, 1, 1).astype(BF16)
+    value_rows = jnp.transpose(joint[0, 2 * D :, :], (1, 0))
+    blank = jnp.zeros((HEAD, AREA), BF16)
+
+    def probs_grads(group):
+        lanes = value_rows[:, group * 128 : (group + 1) * 128]
+        found = []
+        for head in range(4):
+            at = group * 128 + head * HEAD
+            parts = [blank] * 4
+            parts[head] = grad_mixture[at : at + HEAD, :]
+            found.append(dot(lanes, jnp.concatenate(parts, axis=0), 1, 0))
+        return found
+
+    ahead = probs_grads(0)
+    for group in range(HEADS // 4):
+        current = ahead
+        if group + 1 < HEADS // 4:
+            ahead = probs_grads(group + 1)
+        raws = []
+        for i in range(4):
+            head = group * 4 + i
+            weight = probs[0, head].astype(F32)
+            weighted = weight * current[i]
+            grad_scores = weighted - weight * (col_sum(weighted) / col_sum(weight))
+            table_grad[head] += grad_scores
+            raws.append((grad_scores * scale[0, head]).astype(BF16))
+        for i in range(4):
+            at = (group * 4 + i) * HEAD
+            grads_f32[at : at + HEAD, :] = dot(joint[0, D + at : D + at + HEAD, :], raws[i], 1, 0)
+            grads_f32[D + at : D + at + HEAD, :] = dot(joint[0, at : at + HEAD, :], raws[i], 1, 1)
+            joint_grad[2 * D + at : 2 * D + at + HEAD, :] = dot(
+                grad_mixture[at : at + HEAD, :], probs[0, group * 4 + i], 1, 1
+            ).astype(BF16)
+
+    def unit_back(rows, place):
+        shaped = grads_f32[rows, :].reshape(HEADS, HEAD, AREA)
+        unit = joint[0, rows, :].astype(F32).reshape(HEADS, HEAD, AREA)
+        inner = jnp.sum(unit * shaped, axis=1, keepdims=True)
+        shaped = shaped - unit * inner
+        for head in range(HEADS):
+            at = rows.start + head * HEAD
+            joint_grad[at : at + HEAD, :] = (
+                shaped[head] * inverse[0, place + head : place + head + 1, :]
+            ).astype(BF16)
+        return inner
+
+    inner = unit_back(slice(0, D), 0)
     for head in range(HEADS):
-        at = head * HEAD
-        grad_mix = dot(out_weight[at : at + HEAD, :], grad_low, 1, 1)
-        grad_mix = grad_mix.astype(BF16)
-        low = probs[0, head]
-        query = joint[0, at : at + HEAD, :]
-        key = joint[0, D + at : D + at + HEAD, :]
-        value = joint[0, 2 * D + at : 2 * D + at + HEAD, :]
-        weight = low.astype(F32)
-        weighted = weight * dot(value, grad_mix, 0, 0)
-        grad_scores = weighted - weight * (col_sum(weighted) / col_sum(weight))
-        table_grad[head] += grad_scores
-        grad_raw = (grad_scores * scale[0, head]).astype(BF16)
-        grad_query = dot(key, grad_raw, 1, 0)
-        grad_key = dot(query, grad_raw, 1, 1)
-        grad_value = dot(grad_mix, low, 1, 1)
-        query = query.astype(F32)
-        key = key.astype(F32)
-        query_inner = col_sum(query * grad_query)
-        key_inner = col_sum(key * grad_key)
-        scale_grad[head : head + 1, :] += query_inner
-        grad_query = inverse[0, head : head + 1, :] * (grad_query - query * query_inner)
-        grad_key = inverse[0, HEADS + head : HEADS + head + 1, :] * (grad_key - key * key_inner)
-        joint_grad[at : at + HEAD, :] = grad_query.astype(BF16)
-        joint_grad[D + at : D + at + HEAD, :] = grad_key.astype(BF16)
-        joint_grad[2 * D + at : 2 * D + at + HEAD, :] = grad_value.astype(BF16)
+        scale_grad[head : head + 1, :] += inner[head]
+    unit_back(slice(D, 2 * D), HEADS)
     in_grad[...] += dot(win_t[0], joint_grad[...], 1, 1)
     windows[mine, :] = dot(joint_grad[...], in_weight[...], 0, 1)
 
@@ -995,6 +1056,7 @@
             pltpu.VMEM((SIDE, SIDE + WS, D), F32),
             pltpu.VMEM((TOKENS, D), F32),
             pltpu.VMEM((3 * D, AREA), BF16),
+            pltpu.VMEM((2 * D, AREA), F32),
             pltpu.VMEM((D + 16, 3 * D), F32),
             pltpu.VMEM((D, D), F32),
         ],
@@ -1065,13 +1127,13 @@
         values_grad[head : head + 1, :] = col_sum(total)
     f_row, f_col = offsets_row((UNITS, TABLE), 1, -1.0)
     w1t = jnp.transpose(w1[...], (1, 0))
-    b1t = jnp.transpose(b1[...], (1, 0))
+    b1t = jnp.transpose(row_of(b1), (1, 0))
     hidden, slope = gelu_pair(w1t[:, 0:1] * f_row + w1t[:, 1:2] * f_col + b1t[:, 0:1])
-    chance = jax.nn.sigmoid(exact_dot(w2[...], hidden, 0, 0))
+    chance = jax.nn.sigmoid(exact_dot(w2[...], hidden, 1, 0))
     grad_pre = values_grad[:HEADS, :] * (16.0 * chance * (1.0 - chance))
     small[...] = jnp.zeros_like(small)
     put_small(small, places, "table_two", exact_dot(grad_pre, hidden, 1, 1))
-    grad_hidden = exact_dot(w2[...], grad_pre, 1, 0) * slope
+    grad_hidden = exact_dot(w2[...], grad_pre, 0, 0) * slope
     f_row, f_col = offsets_row((8, TABLE), 1, -1.0)
     kind = iota((8, TABLE), 0)
     factors = jnp.where(kind == 0, f_row, jnp.where(kind == 1, f_col, 1.0))
@@ -1159,12 +1221,12 @@
     scale[...] = get("scale")[:, 0:1]
     one = get("table_one")
     table_first[...] = one[0:2, :]
-    table_first_bias[...] = one[2:3, :]
-    table_second[...] = jnp.transpose(get("table_two"), (1, 0))
-    out_bias[...] = get("out_bias")
-    up_bias[...] = get("up_bias")
-    down_bias[...] = get("down_bias")
-    router[...] = jnp.transpose(get("router"), (1, 0))
+    table_first_bias[...] = one[2:3, :].reshape(UNITS)
+    table_second[...] = get("table_two")
+    out_bias[...] = get("out_bias").reshape(D)
+    up_bias[...] = get("up_bias").reshape(FF)
+    down_bias[...] = get("down_bias").reshape(D)
+    router[...] = get("router")
     gain[0:1, :] = get("gain_first")
     gain[1:3, :] = get("gain_rest")
     offset[0:1, :] = get("offset_first")
@@ -1180,15 +1242,15 @@
             full((2, D)),
             full((HEADS, 1)),
             full((2, UNITS)),
-            full((1, UNITS)),
-            full((UNITS, HEADS)),
+            full((UNITS,)),
+            full((HEADS, UNITS)),
             full((D, D)),
-            full((1, D)),
+            full((D,)),
             full((D, FF)),
-            full((1, FF)),
+            full((FF,)),
             full((FF, D)),
-            full((1, D)),
-            full((D, experts)),
+            full((D,)),
+            full((experts, D)),
             full((D, FF)),
             full((1, FF)),
             full((FF, D)),
@@ -1221,31 +1283,31 @@
 
     picture = tokens.reshape(SIDE, SIDE, D)
     cot = cotangent.reshape(SIDE, SIDE, D)
-    route_col = routes.reshape(TOKENS, 1)
-    first_bias = bias_net_first_bias.reshape(1, UNITS)
+    router_t = router_weight.T
+    second_t = bias_net_second_weight.T
 
     slot_col, slot_row, cot_slots, table, scale = prep(
-        route_col, cot, bias_net_first_weight, first_bias, bias_net_second_weight,
-        logit_scale.reshape(1, HEADS), experts, capacity, slots,
+        routes.reshape(1, TOKENS), cot, bias_net_first_weight, bias_net_first_bias, second_t,
+        logit_scale, experts, capacity, slots,
     )
     cot_arrived, normed, n_zero, rstd_zero, joint, probs, mixture, win_t, inverse = attend(
         cot_slots, shifts, scale, picture, in_weight, in_bias, table,
-        out_weight, out_bias.reshape(1, D), norm_gain, norm_bias,
+        out_weight, out_bias, norm_gain, norm_bias,
     )
     first_low, active, slope, n_one, rstd_one, second, buffer = forward(
-        shifts, picture, normed, up_weight, up_bias.reshape(1, FF), down_weight,
-        down_bias.reshape(1, D), norm_gain, norm_bias, slot_row, experts, slots,
+        shifts, picture, normed, up_weight, up_bias, down_weight,
+        down_bias, norm_gain, norm_bias, slot_row, experts, slots,
     )
     returned, grad_returned, own_packed = run_experts(
-        buffer, cot_arrived, router_weight, expert_up[0], expert_up_bias, expert_down[0],
+        buffer, cot_arrived, router_t, expert_up[0], expert_up_bias, expert_down[0],
         expert_down_bias, norm_gain, own_rows,
     )
     (
         result, grad_first, dense_packed, up_bias_grad, down_bias_grad, router_grad,
         gain_grad, offset_grad,
     ) = backward(
-        second, cot, slot_col, route_col, returned.reshape(-1, D), grad_returned.reshape(-1, D),
-        router_weight, first_low, active, slope, n_one, rstd_one, up_weight, down_weight,
+        second, cot, slot_col, returned.reshape(-1, D), grad_returned.reshape(-1, D),
+        router_t, first_low, active, slope, n_one, rstd_one, up_weight, down_weight,
         norm_gain, norm_bias, dense_rows,
     )
     (
@@ -1256,8 +1318,8 @@
         in_weight, out_weight, norm_gain, last_rows,
     )
     small = table_back(
-        small_rows, experts, table_grad, scale_rows, bias_net_first_weight, first_bias,
-        bias_net_second_weight, in_bias_grad, out_bias_grad, up_bias_grad, down_bias_grad,
+        small_rows, experts, table_grad, scale_rows, bias_net_first_weight, bias_net_first_bias,
+        second_t, in_bias_grad, out_bias_grad, up_bias_grad, down_bias_grad,
         gain_zero, gain_grad, offset_zero, offset_grad, router_grad,
     )
     sums = reduce_all(
@@ -1275,15 +1337,15 @@
         in_bias_grad,
         scale_grad.reshape(HEADS),
         table_one,
-        table_bias.reshape(UNITS),
-        table_two,
+        table_bias,
+        table_two.T,
         out_grad,
-        out_bias_grad.reshape(D),
+        out_bias_grad,
         up_grad,
-        up_bias_grad.reshape(FF),
+        up_bias_grad,
         down_grad,
-        down_bias_grad.reshape(D),
-        router_grad,
+        down_bias_grad,
+        router_grad.T,
         own_up[None],
         own_up_bias,
         own_down[None],

time: 388 us -> 305 us (0.79)
  Pallas kernels: 362 us -> 293 us
  local copies, waits for them, and re-layouts: 15.4 us -> 4.95 us
    pallas_call x1, Pallas kernels: 62.1 us -> 28.1 us  [attend(): pl.pallas_call(attend_kernel, grid=(WINDOWS,), in_specs=[pl.BlockSpec(mem...]
    pallas_call x1, Pallas kernels: 63 us -> 29.1 us  [attend_back(): pl.pallas_call(attend_back_kernel, grid=(WINDOWS,), in_specs=[smem(), sme...]
    reshape x4 -> x0, local copies, waits for them, and re-layouts: 5.62 us -> none  [the longest x1 1.84 us: per_device(): route_col = routes.reshape(TOKENS, 1)]
    unnamed x7 -> x1, local copies, waits for them, and re-layouts: 9.74 us -> 4.95 us
where the time goes in v3:
time: 305 us; the launch traced here: 300 us
  Pallas kernels  293 us (96%)
  local copies, waits for them, and re-layouts  4.95 us (2%)
    pallas_call x1, Pallas kernels, reduce_all(): pl.pallas_call(functools.partial(reduce_kernel, names), out_shape=tuple((...  113 us
    pallas_call x1, Pallas kernels, run_experts(): pl.pallas_call(expert_kernel, out_shape=(full(blocks, BF16), full(blocks,...  50 us
    pallas_call x1, Pallas kernels, attend_back(): pl.pallas_call(attend_back_kernel, grid=(WINDOWS,), in_specs=[smem(), sme...  29.1 us
    pallas_call x1, Pallas kernels, attend(): pl.pallas_call(attend_kernel, grid=(WINDOWS,), in_specs=[pl.BlockSpec(mem...  28.1 us
    pallas_call x1, Pallas kernels, backward(): pl.pallas_call(backward_kernel, grid=(TOKENS // ROWS,), in_specs=[rows(D)...  28 us
    pallas_call x1, Pallas kernels, forward(): pl.pallas_call(forward_kernel, grid=(TOKENS // ROWS,), in_specs=[smem(),...  19.1 us
    pallas_call x1, Pallas kernels, prep(): pl.pallas_call(functools.partial(prep_kernel, capacity), out_shape=(full(...  9.49 us
    pallas_call x1, Pallas kernels, table_back(): pl.pallas_call(functools.partial(table_back_kernel, places), out_shape=fu...  8.52 us

profile of v3, /device:TPU:25, one launch (start us, length us, event | category | flops | bytes accessed | tf_op | source)
XLA Modules:
  0.0 299.7 jit_solution(17299399728259897568)
XLA Ops:
  0.7 9.5 %prep.1 = (s32[1296,1]{1,0:T(8,128)}, s32[1,1296]{1,0:T(1,128)}, bf16[4,416,384]{2,1,0:T(8,128)(2,1)}, f32[12,144,144]{2,1,0:T(8,128)}, f32[1,12]{1,0:T(1,128)}) custom-call(s32[1,1296]{1,0:T(1,128)} %bitcast.28, bf16[36,36,384]{2,1,0:T(8,128)(2,1)} %bitcast.17, f32[2,512]{1,0:T(2,128)} %w1.3, f32[512]{0:T(512)} %b1.3, f32[12,512]{1,0:T(8,128)} %bitcast.24, ...), custom_call_target="tpu_custom_call" | custom-call | tf_op jit(solution)/shard_map/prep/pallas_call | solution.py:330
  10.1 28.1 %attend.1 = (bf16[4,416,384]{2,1,0:T(8,128)(2,1)}, f32[1296,384]{1,0:T(8,128)}, bf16[1296,384]{1,0:T(8,128)(2,1)}, f32[1296,1]{1,0:T(8,128)}, bf16[9,1152,144]{2...) custom-call(bf16[4,416,384]{2,1,0:T(8,128)(2,1)} %get-tuple-element., ...), custom_call_target="tpu_custom_call" | custom-call | tf_op jit(solution)/shard_map/attend/pallas_call | solution.py:495
  38.3 19.1 %forward.1 = (bf16[1296,384]{1,0:T(8,128)(2,1)}, bf16[1296,1536]{1,0:T(8,128)(2,1)}, bf16[1296,1536]{1,0:T(8,128)(2,1)}, bf16[1296,384]{1,0:T(8,128)(2,1)}, f32[...) custom-call(s32[1,2]{1,0:T(1,128)} %shifts.5, bf16[36,36,384]{2,1,0:T(8,128)(2,1)} %bitcast.16, ...), custom_call_target="tpu_custom_call" | custom-call | tf_op jit(solution)/shard_map/forward/pallas_call | solution.py:594
  57.4 50.0 %experts.1 = (bf16[4,416,384]{2,1,0:T(8,128)(2,1)}, bf16[4,416,384]{2,1,0:T(8,128)(2,1)}, bf16[3200,384]{1,0:T(8,128)(2,1)}) custom-call(bf16[4,416,384]{2,1,0:T(8,128)(2,1)} %get-tuple-element.91.buffer, bf16[4,416,384]{2,1,0:T(8,128)(2,1)} %get-tuple-element.92.cot, f32[4,384]{1,0:T(4,128)} %bitcast.26, bf16[384,1536]{1,0:T(8,128)(2,1)} %bitcast.22, ...), custom_call_target="tpu_custom_call" | custom-call | tf_op jit(solution)/shard_map/experts/pallas_call | solution.py:758
  107.4 28.0 %backward.1 = (bf16[36,36,384]{2,1,0:T(8,128)(2,1)}, f32[1296,384]{1,0:T(8,128)}, bf16[3072,384]{1,0:T(8,128)(2,1)}, f32[1,1536]{1,0:T(1,128)}, f32[1,384]{1,0:T...) custom-call(f32[1296,384]{1,0:T(8,128)} %get-tuple-element.89.second, ...), custom_call_target="tpu_custom_call" | custom-call | tf_op jit(solution)/shard_map/backward/pallas_call | solution.py:859
  135.4 29.1 %attend_back.1 = (f32[36,36,384]{2,1,0:T(8,128)}, bf16[1536,384]{1,0:T(8,128)(2,1)}, f32[1,1152]{1,0:T(1,128)}, f32[1,384]{1,0:T(1,128)}, f32[1,384]{1,0:T(1,128...) custom-call(s32[1,2]{1,0:T(1,128)} %shifts.5, f32[1,12]{1,0:T(1,128)} %get-tuple-element.85.scale, ...), custom_call_target="tpu_custom_call" | custom-call | tf_op jit(solution)/shard_map/attend_back/pallas_call | solution.py:1017
  164.5 5.0 %copy.45 = f32[1,36,36,384]{3,0,2,1:T(1,128)} copy(f32[1,36,36,384]{3,2,1,0:T(8,128)} %bitcast.19) | data formatting | bytes 3981312
  169.5 8.5 %table_back.1.refs_3_ = f32[256,128]{1,0:T(8,128)} custom-call(f32[12,144,144]{2,1,0:T(8,128)} %get-tuple-element.113.table_grad, f32[12,144]{1,0:T(8,128)} %get-tuple-element.114.scale_rows, f32[2,512]{1,0:T(2,128)} %w1.3, f32[512]{0:T(512)} %b1.3, f32[12,512]{1,0:T(8,128)} %bitcast.25, f32[1,1152]{1,0:T(1,128)} %get-tuple-element.115.in_bias, ...), custom_call_target="tpu_custom_call" | custom-call | tf_op jit(solution)/shard_map/table_back/pallas_call | solution.py:1156
  178.0 112.7 %reduce.2 = (bf16[3200,384]{1,0:T(8,128)(2,1)}, bf16[3072,384]{1,0:T(8,128)(2,1)}, bf16[1536,384]{1,0:T(8,128)(2,1)}, f32[256,128]{1,0:T(8,128)}) custom-call(bf16[3200,384]{1,0:T(8,128)(2,1)} %get-tuple-element.110.refs_0_, bf16[3072,384]{1,0:T(8,128)(2,1)} %get-tuple-element.111.refs_1_, bf16[1536,384]{1,0:T(8,128)(2,1)} %get-tuple-element.112.refs_2_, ...), custom_call_target="tpu_custom_call" | custom-call | tf_op jit(solution)/shard_map/reduce/pallas_call | solution.py:1189
  290.7 7.5 %unpack.1 = (f32[384,1152]{1,0:T(8,128)}, f32[2,384]{1,0:T(2,128)}, f32[12,1]{1,0:T(8,128)}, f32[2,512]{1,0:T(2,128)}, f32[512]{0:T(512)}, /*index=5*/f32[12,512...) custom-call(bf16[3200,384]{1,0:T(8,128)(2,1)} %get-tuple-element.124, ...), custom_call_target="tpu_custom_call" | custom-call | tf_op jit(solution)/shard_map/unpack/pallas_call | solution.py:1238
  298.2 1.3 reduce.1
